TPU v7x, 32 devices: a whole 2x2x4 slice. The times are simulated.
32 devices in a mesh: replica: 8 (over z, core), tensor: 4 (over y, x).
Axes of the slice: x: 2, y: 2, z: 4, core: 2. Of those that a mesh axis runs over, the one named last changes fastest.
Arguments:
- token_ids: int32 [768, 4], P('replica'), may hold values from 0 to 32063, as said below
- cache_lengths: int32 [768], P('replica'), may hold values from 2 to 160, as said below
- embedding: bfloat16 [32064, 8192], P('replica', 'tensor'), may hold values from -15 to 15
- norm_gain: float32 [8192], replicated, may hold values from 0.5 to 1.5
- rotated_key_cache: bfloat16 [768, 160, 1024], P('replica', None, 'tensor'), may hold values from -200 to 200
- stored_value_cache: bfloat16 [768, 160, 1024], P('replica', None, 'tensor'), may hold values from -6 to 6
- teacher_q: float32 [8192, 4096], P(('replica', 'tensor')), may hold values from -0.0625 to 0.0625
- teacher_k: float32 [8192, 1024], P(('replica', 'tensor')), may hold values from -0.0625 to 0.0625
- teacher_v: float32 [8192, 1024], P(('replica', 'tensor')), may hold values from -0.0625 to 0.0625
- teacher_o: float32 [8192, 4096], P(('replica', 'tensor')), may hold values from -0.09375 to 0.09375
- student_q: float32 [8192, 4096], P(('replica', 'tensor')), may hold values from -0.0625 to 0.0625
- student_k: float32 [8192, 1024], P(('replica', 'tensor')), may hold values from -0.0625 to 0.0625
- student_v: float32 [8192, 1024], P(('replica', 'tensor')), may hold values from -0.0625 to 0.0625
- student_o: float32 [8192, 4096], P(('replica', 'tensor')), may hold values from -0.09375 to 0.09375
Outputs:
- next_q: float32 [8192, 4096], P(('replica', 'tensor'))
- next_k: float32 [8192, 1024], P(('replica', 'tensor'))
- next_v: float32 [8192, 1024], P(('replica', 'tensor'))
- next_o: float32 [8192, 4096], P(('replica', 'tensor'))
- hidden_out: bfloat16 [768, 4, 8192], P('replica', None, 'tensor')
Inputs may be any that keep to these rules, and one draw needn't show every extreme that they name: `token_ids`: the 384 ids of one replica's rows fall at most 96 times into one block of 4008 consecutive vocabulary entries, and exactly 96 times into one such block. `cache_lengths`: filled cache slots of a row; slots from it on hold nothing that is read.
All inputs are finite; a program needn't handle non-finite values.
Results may differ from a plain program's by a relative error of at most 0.0076.
Values may be sent and summed in bfloat16 or wider, within the bound.
No kernel may reach another device: no remote copies, remote signals or barrier semaphores. Data moves between devices by JAX's collectives and lax.ppermute only.
A program may use at most 256 MiB of HBM per device.

v0:
```python
import jax
import jax.numpy as jnp
from jax import lax
from jax.sharding import PartitionSpec as P

D = 8192
HEAD_WIDTH = 128
DECODE_STEPS = 4


blend_keep = 0.9
norm_epsilon = 1e-05
rope_theta = 500000.0
masked_score = -1e30


def rotate_half(values, cosine_table, sine_table):
    half_width = values.shape[-1] // 2
    first_half = values[..., :half_width]
    second_half = values[..., half_width:]
    return jnp.concatenate(
        [
            first_half * cosine_table - second_half * sine_table,
            second_half * cosine_table + first_half * sine_table,
        ],
        axis=-1,
    )


def widen_rows(part_rows):
    return lax.all_gather(part_rows, "tensor", axis=2, tiled=True)


def settle_sums(partial_terms):
    return lax.psum_scatter(
        partial_terms.astype(jnp.bfloat16), "tensor", scatter_dimension=2, tiled=True
    ).astype(jnp.float32)


def project_rows(full_rows, norm_gain, weights_q, weights_k, weights_v, cosine_table, sine_table):
    row_count, step_count = (full_rows.shape[0], full_rows.shape[1])
    widened = full_rows.astype(jnp.float32)
    mean_square = jnp.mean(widened * widened, axis=-1, keepdims=True)
    normed = (widened * lax.rsqrt(mean_square + norm_epsilon) * norm_gain).astype(jnp.bfloat16)
    flattened_rows = normed.reshape(row_count * step_count, D)
    query_rows = jnp.dot(flattened_rows, weights_q, preferred_element_type=jnp.float32).reshape(
        row_count, step_count, -1, HEAD_WIDTH
    )
    query_rows = rotate_half(query_rows, cosine_table, sine_table).astype(jnp.bfloat16)
    incoming_keys = jnp.dot(flattened_rows, weights_k, preferred_element_type=jnp.float32).reshape(
        row_count, step_count, -1, HEAD_WIDTH
    )
    incoming_keys = rotate_half(incoming_keys, cosine_table, sine_table).astype(jnp.bfloat16)
    incoming_values = (
        jnp.dot(flattened_rows, weights_v, preferred_element_type=jnp.float32)
        .astype(jnp.bfloat16)
        .reshape(row_count, step_count, -1, HEAD_WIDTH)
    )
    return (query_rows, incoming_keys, incoming_values)


def attend_rows(
    query_rows,
    incoming_keys,
    incoming_values,
    first_step,
    rotated_key_cache,
    stored_value_cache,
    cache_lengths,
):
    row_count, query_steps, query_heads = (
        query_rows.shape[0],
        query_rows.shape[1],
        query_rows.shape[2],
    )
    key_heads, key_steps = (incoming_keys.shape[2], incoming_keys.shape[1])
    slot_count = rotated_key_cache.shape[1]
    query_group_width = query_heads // key_heads
    score_scale = HEAD_WIDTH ** (-0.5)
    grouped_queries = query_rows.reshape(
        row_count, query_steps, key_heads, query_group_width, HEAD_WIDTH
    )
    cached_key_rows = rotated_key_cache.reshape(row_count, slot_count, key_heads, HEAD_WIDTH)
    cached_value_rows = stored_value_cache.reshape(row_count, slot_count, key_heads, HEAD_WIDTH)
    cache_scores = (
        jnp.einsum(
            "rsgqd,rcgd->rsgqc",
            grouped_queries,
            cached_key_rows,
            preferred_element_type=jnp.float32,
        )
        * score_scale
    )
    cache_valid = jnp.arange(slot_count, dtype=jnp.int32)[None, :] < cache_lengths[:, None]
    cache_scores = jnp.where(cache_valid[:, None, None, None, :], cache_scores, masked_score)
    fresh_scores = (
        jnp.einsum(
            "rsgqd,rtgd->rsgqt", grouped_queries, incoming_keys, preferred_element_type=jnp.float32
        )
        * score_scale
    )
    query_index = first_step + jnp.arange(query_steps, dtype=jnp.int32)
    fresh_valid = jnp.arange(key_steps, dtype=jnp.int32)[None, :] <= query_index[:, None]
    fresh_scores = jnp.where(fresh_valid[None, :, None, None, :], fresh_scores, masked_score)
    highest = jnp.maximum(jnp.max(cache_scores, axis=-1), jnp.max(fresh_scores, axis=-1))[..., None]
    cache_exp = jnp.exp(cache_scores - highest)
    fresh_exp = jnp.exp(fresh_scores - highest)
    totals = (jnp.sum(cache_exp, axis=-1) + jnp.sum(fresh_exp, axis=-1))[..., None]
    cache_probs = (cache_exp / totals).astype(jnp.bfloat16)
    fresh_probs = (fresh_exp / totals).astype(jnp.bfloat16)
    attended = jnp.einsum(
        "rsgqc,rcgd->rsgqd", cache_probs, cached_value_rows, preferred_element_type=jnp.float32
    )
    attended = attended + jnp.einsum(
        "rsgqt,rtgd->rsgqd", fresh_probs, incoming_values, preferred_element_type=jnp.float32
    )
    return attended.astype(jnp.bfloat16).reshape(row_count * query_steps, query_heads * HEAD_WIDTH)


def finish_rows(attended, weights_o, local_rows):
    row_count, step_count = (local_rows.shape[0], local_rows.shape[1])
    partial_terms = lax.dot_general(
        attended, weights_o, (((1,), (1,)), ((), ())), preferred_element_type=jnp.float32
    )
    summed = settle_sums(partial_terms.reshape(row_count, step_count, D))
    return (local_rows.astype(jnp.float32) + summed).astype(jnp.bfloat16)


def body(
    token_ids,
    cache_lengths,
    embedding,
    norm_gain,
    rotated_key_cache,
    stored_value_cache,
    teacher_q,
    teacher_k,
    teacher_v,
    teacher_o,
    student_q,
    student_k,
    student_v,
    student_o,
):
    next_q = blend_keep * teacher_q + (1.0 - blend_keep) * student_q
    next_k = blend_keep * teacher_k + (1.0 - blend_keep) * student_k
    next_v = blend_keep * teacher_v + (1.0 - blend_keep) * student_v
    next_o = blend_keep * teacher_o + (1.0 - blend_keep) * student_o
    low_blocks = (
        next_q.astype(jnp.bfloat16),
        next_k.astype(jnp.bfloat16),
        next_v.astype(jnp.bfloat16),
        next_o.astype(jnp.bfloat16),
    )
    moved = (
        lax.all_to_all(low_blocks[0], "tensor", split_axis=1, concat_axis=0, tiled=True),
        lax.all_to_all(low_blocks[1], "tensor", split_axis=1, concat_axis=0, tiled=True),
        lax.all_to_all(low_blocks[2], "tensor", split_axis=1, concat_axis=0, tiled=True),
        lax.all_to_all(low_blocks[3], "tensor", split_axis=1, concat_axis=0, tiled=True),
    )
    sampler = (
        lax.all_gather(moved[0], "replica", axis=0, tiled=True),
        lax.all_gather(moved[1], "replica", axis=0, tiled=True),
        lax.all_gather(moved[2], "replica", axis=0, tiled=True),
        lax.all_gather(moved[3], "replica", axis=0, tiled=True),
    )
    weights_q, weights_k, weights_v, weights_o = sampler
    shard_rows = embedding.shape[0]
    row_count, step_count = (token_ids.shape[0], token_ids.shape[1])
    all_ids = lax.all_gather(token_ids, "replica", axis=0, tiled=True)
    local_ids = all_ids - lax.axis_index("replica") * shard_rows
    inside = (local_ids >= 0) & (local_ids < shard_rows)
    picked = jnp.take(embedding, jnp.clip(local_ids, 0, shard_rows - 1), axis=0)
    terms = jnp.where(inside[..., None], picked.astype(jnp.float32), 0.0)
    local_rows = lax.psum_scatter(
        terms.astype(jnp.bfloat16), "replica", scatter_dimension=0, tiled=True
    )
    positions = (cache_lengths[:, None] + jnp.arange(step_count, dtype=jnp.int32)[None, :]).astype(
        jnp.float32
    )
    inverse = rope_theta ** (-(jnp.arange(HEAD_WIDTH // 2, dtype=jnp.float32) * 2.0) / HEAD_WIDTH)
    angles = positions[:, :, None] * inverse
    cosine_table = jnp.cos(angles)[:, :, None, :]
    sine_table = jnp.sin(angles)[:, :, None, :]
    key_parts = []
    value_parts = []
    results = []
    for step_index in range(DECODE_STEPS):
        step_rows = local_rows[:, step_index : step_index + 1]
        full_rows = widen_rows(step_rows)
        query_rows, incoming_keys, incoming_values = project_rows(
            full_rows,
            norm_gain,
            weights_q,
            weights_k,
            weights_v,
            cosine_table[:, step_index : step_index + 1],
            sine_table[:, step_index : step_index + 1],
        )
        key_parts.append(incoming_keys)
        value_parts.append(incoming_values)
        attended = attend_rows(
            query_rows,
            jnp.concatenate(key_parts, axis=1),
            jnp.concatenate(value_parts, axis=1),
            step_index,
            rotated_key_cache,
            stored_value_cache,
            cache_lengths,
        )
        results.append(finish_rows(attended, weights_o, step_rows))
    hidden_out = jnp.concatenate(results, axis=1)
    return (next_q, next_k, next_v, next_o, hidden_out)


def solution(mesh):
    return jax.shard_map(
        body,
        mesh=mesh,
        in_specs=(
            P("replica", None),
            P("replica"),
            P("replica", "tensor"),
            P(),
            P("replica", None, "tensor"),
            P("replica", None, "tensor"),
            P(("replica", "tensor"), None),
            P(("replica", "tensor"), None),
            P(("replica", "tensor"), None),
            P(("replica", "tensor"), None),
            P(("replica", "tensor"), None),
            P(("replica", "tensor"), None),
            P(("replica", "tensor"), None),
            P(("replica", "tensor"), None),
        ),
        out_specs=(
            P(("replica", "tensor"), None),
            P(("replica", "tensor"), None),
            P(("replica", "tensor"), None),
            P(("replica", "tensor"), None),
            P("replica", None, "tensor"),
        ),
        check_vma=False,
    )
```

profile of v0, /device:TPU:0, one launch (start us, length us, event | category | flops | bytes accessed | tf_op | source)
XLA Modules:
  0.0 955.0 jit_solution(2828573758661802393)
XLA Ops:
  7.2 14.5 %all-gather = s32[8,96,4]{1,2,0:T(4,128)S(1)} all-gather(s32[1,96,4]{1,2,0:T(4,128)} %bitcast.416), channel_id=1, replica_groups=mesh['replica'=8,'tensor'=4] {'replica'}, dimensions={0}, use_global_device_ids=true | all-gather | bytes 13824 | tf_op jit(solution)/shard_map/all_gather | solution.py:170
  22.3 31.6 %gather_fusion = bf16[3072,2048]{1,0:T(8,128)(2,1)} fusion(bf16[4008,2048]{1,0:T(8,128)(2,1)} %param.16, s32[3072]{0:T(1024)S(1)} %broadcast_clamp_fusion), kind=kCustom, calls=%fused_computation | custom fusion | bytes 25178112 | tf_op jit(solution)/shard_map/jit(_take)/gather | solution.py:173
  53.9 19.0 %reshape.749 = bf16[768,4,2048]{2,1,0:T(4,128)(2,1)} reshape(bf16[3072,2048]{1,0:T(8,128)(2,1)} %gather_fusion) | data formatting | bytes 25165824 | tf_op jit(solution)/shard_map/jit(_take)/gather | solution.py:173
  73.0 16.0 %select_convert_fusion = bf16[768,4,2048]{2,0,1:T(8,128)(2,1)} fusion(bf16[768,4,2048]{2,1,0:T(4,128)(2,1)} %reshape.749, pred[768,4]{0,1:T(4,128)(4,1)S(1)} %compare_and_fusion.1, pred[768,4]{0,1:T(4,128)(4,1)S(1)} %reshape.769), kind=kLoop, calls=%fused_computation.1 | loop fusion | flops 25165824 | bytes 25171968 | tf_op jit(solution)/shard_map/convert_element_type | solution.py:176
  89.1 129.1 %reduce-scatter.6.cloned.1.call-done = bf16[96,4,2048]{2,0,1:T(8,128)(2,1)} async-done(((bf16[768,4,2048]{2,0,1:T(8,128)(2,1)}), bf16[96,4,2048]{2,0,1:T(8,128)(2,1)}) %reduce-scatter.6.cloned.1.call-update) | async-done | bytes 1572880 | tf_op jit(solution)/shard_map/reduce_scatter | solution.py:175
  218.1 2.6 fusion.246
  221.5 1.2 fusion.243
  222.7 14.3 %all_to_all.76 = bf16[256,4,256]{0,2,1:T(8,128)(2,1)S(1)} all-to-all(bf16[256,4,256]{0,2,1:T(8,128)(2,1)S(1)} %bitcast.400), channel_id=1, replica_groups=mesh['replica'=8,'tensor'=4] {'tensor'}, dimensions={1} | all-to-all | bytes 1048576 | tf_op jit(solution)/shard_map/all_to_all | solution.py:158
  240.2 1.6 copy.247
  241.7 1.2 fusion.244
  242.9 12.4 %all_to_all.77 = bf16[256,4,256]{0,2,1:T(8,128)(2,1)S(1)} all-to-all(bf16[256,4,256]{0,2,1:T(8,128)(2,1)S(1)} %bitcast.401), channel_id=1, replica_groups=mesh['replica'=8,'tensor'=4] {'tensor'}, dimensions={1} | all-to-all | bytes 1048576 | tf_op jit(solution)/shard_map/all_to_all | solution.py:157
  256.2 5.6 copy.244
  261.8 5.6 copy.245
  267.4 6.2 fusion.245
  273.7 18.0 %all_to_all.78 = bf16[256,4,1024]{0,2,1:T(8,128)(2,1)S(1)} all-to-all(bf16[256,4,1024]{0,2,1:T(8,128)(2,1)S(1)} %bitcast.394), channel_id=1, replica_groups=mesh['replica'=8,'tensor'=4] {'tensor'}, dimensions={1} | all-to-all | bytes 4194304 | tf_op jit(solution)/shard_map/all_to_all | solution.py:156
  291.7 1.7 copy.305
  293.4 5.6 copy.250
  299.0 5.6 copy.251
  304.6 6.2 fusion.242
  310.9 21.8 %all_to_all.79 = bf16[256,4,1024]{0,2,1:T(8,128)(2,1)S(1)} all-to-all(bf16[256,4,1024]{0,2,1:T(8,128)(2,1)S(1)} %bitcast.395), channel_id=1, replica_groups=mesh['replica'=8,'tensor'=4] {'tensor'}, dimensions={1} | all-to-all | bytes 4194304 | tf_op jit(solution)/shard_map/all_to_all | solution.py:159
  332.7 2.4 copy.267
  339.3 1.9 fusion.28
  341.3 3.5 fusion.142
  346.1 1.8 fusion.31
  347.9 3.5 fusion.145
  352.1 36.4 %all-gather.22.cloned.1.call-done = bf16[96,1,8192]{2,0,1:T(8,128)(2,1)} async-done(((bf16[96,1,2048]{2,0,1:T(8,128)(2,1)}), bf16[96,1,8192]{2,0,1:T(8,128)(2,1)}) %all-gather.22.cloned.1.call-update) | async-done | bytes 1572880 | tf_op jit(solution)/shard_map/all_gather | solution.py:31
  388.5 1.8 fusion.34
  390.4 3.5 fusion.148
  394.6 26.7 %all-gather.24.cloned.1.call-done = bf16[96,1,8192]{2,0,1:T(8,128)(2,1)} async-done(((bf16[96,1,2048]{2,0,1:T(8,128)(2,1)}), bf16[96,1,8192]{2,0,1:T(8,128)(2,1)}) %all-gather.24.cloned.1.call-update) | async-done | bytes 1572880 | tf_op jit(solution)/shard_map/all_gather | solution.py:31
  421.3 1.8 fusion.37
  423.1 3.6 fusion.151
  427.4 43.2 %all-gather.14.cloned.1.call-done = bf16[8192,256]{0,1:T(8,128)(2,1)} async-done(((bf16[1024,256]{0,1:T(8,128)(2,1)}), bf16[8192,256]{0,1:T(8,128)(2,1)}) %all-gather.14.cloned.1.call-update) | async-done | bytes 4194320 | tf_op jit(solution)/shard_map/all_gather | solution.py:163
  470.6 3.8 fusion.130
  475.2 1.5 fusion.133
  477.6 1.4 fusion.136
  479.9 1.4 fusion.139
  482.3 139.7 %all-gather.12.cloned.1.call-done = bf16[8192,1024]{0,1:T(8,128)(2,1)} async-done(((bf16[1024,1024]{0,1:T(8,128)(2,1)}), bf16[8192,1024]{0,1:T(8,128)(2,1)}) %all-gather.12.cloned.1.call-update) | async-done | bytes 16777232 | tf_op jit(solution)/shard_map/all_gather | solution.py:162
  622.1 9.5 fusion.111
  631.6 1.2 subtract_convert_fusion
  633.0 2.2 fusion.253
  635.3 7.8 fusion.252
  644.3 2.2 fusion.97
  647.5 126.1 %all-gather.18.cloned.1.call-done = bf16[8192,1024]{1,0:T(8,128)(2,1)} async-done(((bf16[1024,1024]{1,0:T(8,128)(2,1)}), bf16[8192,1024]{1,0:T(8,128)(2,1)}) %all-gather.18.cloned.1.call-update) | async-done | bytes 16777232 | tf_op jit(solution)/shard_map/all_gather | solution.py:165
  773.6 12.2 %fusion.3 = bf16[96,1,8192]{2,0,1:T(8,128)(2,1)} fusion(bf16[96,1024]{1,0:T(8,128)(2,1)S(1)} %reshape.746, bf16[8192,1024]{1,0:T(8,128)(2,1)} %all-gather.18.cloned.1.call-done), kind=kOutput, calls=%fused_computation.10 | convolution fusion | flops 1611399168 | bytes 18546688 | tf_op jit(solution)/shard_map/dot_general | solution.py:122
  785.8 9.6 %fusion.108 = f32[96,1,8,128]{3,0,2,1:T(8,128)S(1)} fusion(bf16[8,128,8192]{2,1,0:T(8,128)(2,1)} %bitcast.391, bf16[96,1,8192]{2,0,1:T(8,128)(2,1)} %all-gather.22.cloned.1.call-done, f32[96]{0:T(128)S(1)} %add_rsqrt_fusion.1, f32[8192]{0:T(1024)} %param.17), kind=kOutput, calls=%fused_computation.103 | convolution fusion | flops 1613758464 | bytes 18776448 | tf_op jit(solution)/shard_map/dot_general | solution.py:46
  795.4 1.0 subtract_convert_fusion.1
  796.6 7.8 fusion.250
  807.7 9.3 fusion.105
  817.1 5.8 fusion.94
  825.0 7.6 fusion.248
  833.6 12.1 %fusion.2 = bf16[96,1,8192]{2,0,1:T(8,128)(2,1)} fusion(bf16[96,1024]{1,0:T(8,128)(2,1)S(1)} %reshape.741, bf16[8192,1024]{1,0:T(8,128)(2,1)} %all-gather.18.cloned.1.call-done), kind=kOutput, calls=%fused_computation.9 | convolution fusion | flops 1611399168 | bytes 18546688 | tf_op jit(solution)/shard_map/dot_general | solution.py:122
  846.1 5.5 fusion.91
  852.3 8.9 fusion.102
  861.7 12.2 %fusion.1 = bf16[96,1,8192]{2,0,1:T(8,128)(2,1)} fusion(bf16[96,1024]{1,0:T(8,128)(2,1)S(1)} %reshape.736, bf16[8192,1024]{1,0:T(8,128)(2,1)} %all-gather.18.cloned.1.call-done), kind=kOutput, calls=%fused_computation.8 | convolution fusion | flops 1611399168 | bytes 18546688 | tf_op jit(solution)/shard_map/dot_general | solution.py:122
  874.2 7.6 fusion.247
  883.7 5.7 fusion.126
  889.5 12.5 %fusion = bf16[96,1,8192]{2,0,1:T(8,128)(2,1)} fusion(bf16[96,1024]{1,0:T(8,128)(2,1)S(1)} %reshape.730, bf16[8192,1024]{1,0:T(8,128)(2,1)} %all-gather.18.cloned.1.call-done), kind=kOutput, calls=%fused_computation.7 | convolution fusion | flops 1611399168 | bytes 18546688 | tf_op jit(solution)/shard_map/dot_general | solution.py:122
  902.1 5.9 copy.294
  907.9 5.7 copy.297
  913.6 2.6 copy.295
  916.3 1.3 copy.296
  917.6 26.2 %reduce-scatter.8.cloned.1.call-done = bf16[96,1,2048]{2,0,1:T(8,128)(2,1)} async-done(((bf16[96,1,8192]{2,0,1:T(8,128)(2,1)}), bf16[96,1,2048]{2,0,1:T(8,128)(2,1)}) %reduce-scatter.8.cloned.1.call-update) | async-done | bytes 393232 | tf_op jit(solution)/shard_map/reduce_scatter | solution.py:35
  943.7 1.9 add_convert_fusion.3
  945.9 2.4 copy.298
  (214 shorter events, 29.3 us)
Async XLA Ops:
  7.2 211.0 %reduce-scatter.6.cloned.1.call-start = ((), (), s32[]{:S(2)}) async-start(), calls=%async_computation.9 | async-start | bytes 14155776 | tf_op jit(solution)/shard_map/reduce_scatter | solution.py:175
  89.0 131.8 %copy-start.6 = (f32[256,1024]{1,0:T(8,128)S(1)}, f32[256,1024]{1,0:T(8,128)}, u32[]{:S(2)}) copy-start(f32[256,1024]{1,0:T(8,128)} %param.22) | copy-start | bytes 3145732
  89.0 132.1 %copy-start.7 = (f32[256,1024]{1,0:T(8,128)S(1)}, f32[256,1024]{1,0:T(8,128)}, u32[]{:S(2)}) copy-start(f32[256,1024]{1,0:T(8,128)} %param.26) | copy-start | bytes 3145732
  89.0 250.3 %all-gather.10.cloned.1.call-start = ((), (), s32[]{:S(2)}) async-start(), calls=%async_computation.10 | async-start | bytes 1966080 | tf_op jit(solution)/shard_map/all_gather | solution.py:31
  220.8 120.5 %all-gather.16.cloned.1.call-start = ((), (), s32[]{:S(2)}) async-start(), calls=%async_computation.13 | async-start | bytes 4718592 | tf_op jit(solution)/shard_map/all_gather | solution.py:164
  221.5 18.3 %copy-start.8 = (f32[256,1024]{1,0:T(8,128)S(1)}, f32[256,1024]{1,0:T(8,128)}, u32[]{:S(2)}) copy-start(f32[256,1024]{1,0:T(8,128)} %param.21) | copy-start | bytes 3145732
  238.0 108.1 %all-gather.20.cloned.1.call-start = ((), (), s32[]{:S(2)}) async-start(), calls=%async_computation.16 | async-start | bytes 1966080 | tf_op jit(solution)/shard_map/all_gather | solution.py:31
  238.6 149.9 %all-gather.22.cloned.1.call-start = ((), (), s32[]{:S(2)}) async-start(), calls=%async_computation.18 | async-start | bytes 1966080 | tf_op jit(solution)/shard_map/all_gather | solution.py:31
  239.2 182.1 %all-gather.24.cloned.1.call-start = ((), (), s32[]{:S(2)}) async-start(), calls=%async_computation.20 | async-start | bytes 1966080 | tf_op jit(solution)/shard_map/all_gather | solution.py:31
  239.8 230.8 %all-gather.14.cloned.1.call-start = ((), (), s32[]{:S(2)}) async-start(), calls=%async_computation.12 | async-start | bytes 4718592 | tf_op jit(solution)/shard_map/all_gather | solution.py:163
  256.1 365.9 %all-gather.12.cloned.1.call-start = ((), (), s32[]{:S(2)}) async-start(), calls=%async_computation.11 | async-start | bytes 18874368 | tf_op jit(solution)/shard_map/all_gather | solution.py:162
  293.4 480.2 %all-gather.18.cloned.1.call-start = ((), (), s32[]{:S(2)}) async-start(), calls=%async_computation.14 | async-start | bytes 18874368 | tf_op jit(solution)/shard_map/all_gather | solution.py:165
  332.7 4.5 copy-start.44
  335.1 6.2 copy-start.12
  335.1 582.5 %reduce-scatter.14.cloned.1.call-start = ((), (), s32[]{:S(2)}) async-start(), calls=%async_computation.21 | async-start | bytes 1966080 | tf_op jit(solution)/shard_map/reduce_scatter | solution.py:35
  339.3 135.2 %copy-start.14 = (f32[96,64]{1,0:T(8,128)}, f32[96,64]{1,0:T(8,128)S(1)}, u32[]{:S(2)}) copy-start(f32[96,64]{1,0:T(8,128)S(1)} %get-tuple-element.65) | copy-start | bytes 73732
  339.3 135.2 %copy-start.16 = (f32[96,64]{1,0:T(8,128)}, f32[96,64]{1,0:T(8,128)S(1)}, u32[]{:S(2)}) copy-start(f32[96,64]{1,0:T(8,128)S(1)} %get-tuple-element.96) | copy-start | bytes 73732
  339.3 137.5 %copy-start.18 = (f32[96,64]{1,0:T(8,128)}, f32[96,64]{1,0:T(8,128)S(1)}, u32[]{:S(2)}) copy-start(f32[96,64]{1,0:T(8,128)S(1)} %get-tuple-element.68) | copy-start | bytes 73732
  339.3 137.5 %copy-start.20 = (f32[96,64]{1,0:T(8,128)}, f32[96,64]{1,0:T(8,128)S(1)}, u32[]{:S(2)}) copy-start(f32[96,64]{1,0:T(8,128)S(1)} %get-tuple-element.93) | copy-start | bytes 73732
  339.3 139.8 %copy-start.22 = (f32[96,64]{1,0:T(8,128)}, f32[96,64]{1,0:T(8,128)S(1)}, u32[]{:S(2)}) copy-start(f32[96,64]{1,0:T(8,128)S(1)} %get-tuple-element.67) | copy-start | bytes 73732
  339.3 139.8 %copy-start.23 = (f32[96,64]{1,0:T(8,128)}, f32[96,64]{1,0:T(8,128)S(1)}, u32[]{:S(2)}) copy-start(f32[96,64]{1,0:T(8,128)S(1)} %get-tuple-element.94) | copy-start | bytes 73732
  339.3 142.1 %copy-start.24 = (f32[96,64]{1,0:T(8,128)}, f32[96,64]{1,0:T(8,128)S(1)}, u32[]{:S(2)}) copy-start(f32[96,64]{1,0:T(8,128)S(1)} %get-tuple-element.66) | copy-start | bytes 73732
  423.1 47.5 %copy-start.1 = (bf16[96,1,8192]{2,0,1:T(8,128)(2,1)S(1)}, bf16[96,1,8192]{2,0,1:T(8,128)(2,1)}, u32[]{:S(2)}) copy-start(bf16[96,1,8192]{2,0,1:T(8,128)(2,1)} %all-gather.10.cloned.1.call-done) | copy-start | bytes 4718596
  470.6 4.6 copy-start.2
  470.6 4.6 copy-start.45
  475.2 2.3 copy-start.3
  477.6 2.4 copy-start.4
  479.9 1.5 copy-start.25
  631.6 3.7 copy-start.41
  631.6 12.6 %slice-start = ((s8[7864320]{0:T(1024)(128)(4,1)}), s8[4194304]{0:T(1024)(128)(4,1)S(1)}, s32[]{:S(2)}) async-start(s8[7864320]{0:T(1024)(128)(4,1)} %bitcast.417), calls=%async_computation.22 | async-start | bytes 8388608
  635.3 9.0 slice-start.1
  644.3 2.3 copy-start.30
  644.3 2.2 copy-start.32
  644.3 2.3 copy-start.35
  644.3 2.3 copy-start.37
  785.8 131.8 %reduce-scatter.12.cloned.1.call-start = ((), (), s32[]{:S(2)}) async-start(), calls=%async_computation.19 | async-start | bytes 1966080 | tf_op jit(solution)/shard_map/reduce_scatter | solution.py:35
  796.6 7.9 copy-start.28
  796.6 7.9 copy-start.47
  804.5 2.5 copy-start.11
  805.2 0.7 copy-start.26
  805.3 1.7 copy-start.9
  817.0 5.9 copy-start.10
  817.0 5.9 copy-start.27
  817.0 5.9 copy-start.31
  817.0 5.9 copy-start.33
  817.1 5.9 copy-start.36
  817.1 5.9 copy-start.39
  822.9 0.9 copy-start.19
  822.9 0.9 copy-start.21
  823.0 1.3 copy-start.38
  823.0 1.3 copy-start.46
  823.8 1.2 copy-start.42
  845.8 71.8 %reduce-scatter.10.cloned.1.call-start = ((), (), s32[]{:S(2)}) async-start(), calls=%async_computation.17 | async-start | bytes 1966080 | tf_op jit(solution)/shard_map/reduce_scatter | solution.py:35
  846.1 5.5 copy-start.34
  851.6 0.8 copy-start.13
  852.3 8.9 copy-start.15
  852.3 8.9 copy-start.17
  861.7 12.5 %copy-start.43 = (pred[96,160]{1,0:T(8,128)(4,1)S(1)}, pred[96,160]{1,0:T(8,128)(4,1)}, u32[]{:S(2)}) copy-start(pred[96,160]{1,0:T(8,128)(4,1)} %iota_compare_fusion) | copy-start | bytes 46084
  873.9 7.9 copy-start.40
  873.9 9.7 %copy-start.29 = (f32[96,2,128]{2,1,0:T(2,128)S(1)}, f32[96,2,128]{2,1,0:T(2,128)}, u32[]{:S(2)}) copy-start(f32[96,2,128]{2,1,0:T(2,128)} %reshape.747) | copy-start | bytes 294916
  874.0 69.8 %reduce-scatter.8.cloned.1.call-start = ((), (), s32[]{:S(2)}) async-start(), calls=%async_computation.15 | async-start | bytes 1966080 | tf_op jit(solution)/shard_map/reduce_scatter | solution.py:35
  907.9 8.4 copy-start.5
  913.6 30.1 %copy-start = (bf16[96,4,2048]{2,0,1:T(8,128)(2,1)S(1)}, bf16[96,4,2048]{2,0,1:T(8,128)(2,1)}, u32[]{:S(2)}) copy-start(bf16[96,4,2048]{2,0,1:T(8,128)(2,1)} %reduce-scatter.6.cloned.1.call-done) | copy-start | bytes 4718596
Sparse Core Ops, SparseCore 0:
  89.1 128.9 reduce-scatter.5
  220.9 34.1 all-gather.9
  257.2 48.8 all-gather.15
  307.8 34.9 all-gather.19
  344.5 43.9 all-gather.21
  390.2 30.9 all-gather.23
  423.4 47.1 all-gather.13
  472.2 149.8 all-gather.11
  624.3 149.2 all-gather.17
  785.9 29.1 reduce-scatter.13
  845.9 29.4 reduce-scatter.11
  878.3 31.0 reduce-scatter.9
  912.9 30.8 reduce-scatter.7
where the time goes:
time: 966 us; the launch traced here: 955 us
  waiting for transfers between devices  529 us (55%)
  matrix products  165 us (17%)
  local copies, waits for them, and re-layouts  109 us (11%)
  blocking collectives  81 us (8%)
  other arithmetic  54.1 us (6%)
  between operations  15.3 us (2%)
    all_gather x1, waiting for transfers between devices, body(): lax.all_gather(moved[0], 'replica', axis=0, tiled=True)  140 us
    reduce_scatter x1, waiting for transfers between devices, body(): lax.psum_scatter(terms.astype(jnp.bfloat16), 'replica', scatter_dimension...  129 us
    all_gather x1, waiting for transfers between devices, body(): lax.all_gather(moved[3], 'replica', axis=0, tiled=True)  126 us
    all_gather x4, waiting for transfers between devices, widen_rows(): return lax.all_gather(part_rows, 'tensor', axis=2, tiled=True)  63.1 us
    gather x2, local copies, waits for them, and re-layouts, body(): picked = jnp.take(embedding, jnp.clip(local_ids, 0, shard_rows - 1), axis=0)  50.6 us
    dot_general x4, matrix products, finish_rows(): lax.dot_general(attended, weights_o, (((1,), (1,)), ((), ())), preferred_...  49 us
    unnamed x113, local copies, waits for them, and re-layouts  43.8 us
    all_gather x1, waiting for transfers between devices, body(): lax.all_gather(moved[1], 'replica', axis=0, tiled=True)  43.2 us
  transfers between devices with their start and end apart: 13, of which 7 were waited for; matrix products, arithmetic and copies ran while one was open for 25% of the time, Pallas kernels for 0%

commit v1 on v0

v1 whole, which is shorter than its diff:
```python
import functools

import jax
import jax.numpy as jnp
import numpy as np
from jax import lax
from jax.experimental import pallas as pl
from jax.experimental.pallas import tpu as pltpu
from jax.sharding import PartitionSpec as P

D = 8192
HEAD_WIDTH = 128
DECODE_STEPS = 4
CORES = 2

blend_keep = 0.9
norm_epsilon = 1e-05
rope_theta = 500000.0
masked_score = -1e30

VMEM = 60 * 1024 * 1024

f32 = jnp.float32
bf16 = jnp.bfloat16


def swap(values, bits, count):
    return lax.ppermute(values, "tensor", [(i, i ^ bits) for i in range(count)])


def pass_kernel(values_ref, other_ref, out_ref):
    pass


def after(values, other):
    anywhere = pl.BlockSpec(memory_space=pl.ANY)
    return pl.pallas_call(
        pass_kernel,
        in_specs=[anywhere, anywhere],
        out_specs=anywhere,
        out_shape=jax.ShapeDtypeStruct(values.shape, values.dtype),
        input_output_aliases={0: 0},
        cost_estimate=pl.CostEstimate(flops=0, bytes_accessed=0, transcendentals=0),
    )(values, other)


def due_order(count):
    if count == 4:
        order = [[3, 2, 1, 0], [0, 3, 2, 1], [3, 0, 1, 2], [0, 1, 2, 3]]
    else:
        order = [
            sorted(range(count), key=lambda d, z=z: (d == z, -abs(d - z))) for z in range(count)
        ]
    return np.array(order, dtype=np.int32)


def line_sum(products, place, count, gates):
    if count == 4:
        first, second, third, own = products
        one = lax.ppermute(first, "z", [(0, 1), (3, 2)])
        one = after(one, gates[0])
        block = (second.astype(f32) + one.astype(f32)).astype(bf16)
        up = lax.ppermute(block, "z", [(0, 1), (1, 2)])
        down = lax.ppermute(block, "z", [(3, 2), (2, 1)])
        up = after(up, gates[1])
        rest = jnp.where(place == 2, first, third).astype(f32)
        block = (rest + up.astype(f32)).astype(bf16)
        up = lax.ppermute(block, "z", [(0, 1), (1, 2), (2, 3)])
        rest = jnp.where(place == 1, first, third).astype(f32)
        block = (rest + down.astype(f32)).astype(bf16)
        down = lax.ppermute(block, "z", [(3, 2), (2, 1), (1, 0)])
        return own, up, down
    order = due_order(count)
    arrived = [None, None]
    for step in range(1, count):
        for way, sign in enumerate((1, -1)):
            sources = [z for z in range(count) if 0 <= z + sign * (count - step) < count]
            picks = {z: int(np.where(order[z] == z + sign * (count - step))[0][0]) for z in sources}
            names = sorted(set(picks.values()))
            block = products[names[0]].astype(f32)
            for name in names[1:]:
                chosen = functools.reduce(
                    jnp.logical_or, [place == z for z in sources if picks[z] == name]
                )
                block = jnp.where(chosen, products[name].astype(f32), block)
            if arrived[way] is not None:
                block = block + arrived[way].astype(f32)
            pairs = [(z, z + sign) for z in sources if 0 <= z + sign < count]
            arrived[way] = lax.ppermute(block.astype(bf16), "z", pairs)
    return products[-1], arrived[0], arrived[1]


def line_gather(block, count):
    blocks = {0: block}
    up = down = block
    for step in range(1, count):
        up = lax.ppermute(up, "z", [(i, i + 1) for i in range(step - 1, count - 1)])
        down = lax.ppermute(down, "z", [(i, i - 1) for i in range(1, count - step + 1)])
        blocks[-step], blocks[step] = up, down
    return blocks


def blend_kernel(widths, place_ref, *refs):
    count = len(widths)
    teachers, students = refs[:count], refs[count : 2 * count]
    nexts, lows = refs[2 * count : 3 * count], refs[3 * count :]
    step = pl.program_id(0)
    start = 0
    for teacher, student, following, width in zip(teachers, students, nexts, widths):
        value = blend_keep * teacher[...] + (1.0 - blend_keep) * student[...]
        following[...] = value
        for bits, low in enumerate(lows):

            @pl.when(step == bits)
            def _(low=low, value=value, start=start, width=width):
                low[:, start : start + width] = value.astype(bf16)

        start += width


def blend(teachers, students, place, count):
    height = teachers[0].shape[0]
    widths = [x.shape[1] // count for x in teachers]
    columns = [
        pl.BlockSpec((height, width), lambda i, ref: (0, jnp.bitwise_xor(i, ref[0])))
        for width in widths
    ]
    low = pl.BlockSpec((height, sum(widths)), lambda i, ref: (0, 0))
    results = pl.pallas_call(
        functools.partial(blend_kernel, widths),
        grid_spec=pltpu.PrefetchScalarGridSpec(
            num_scalar_prefetch=1,
            grid=(count,),
            in_specs=columns * 2,
            out_specs=columns + [low] * count,
        ),
        out_shape=[jax.ShapeDtypeStruct(x.shape, f32) for x in teachers]
        + [jax.ShapeDtypeStruct((height, sum(widths)), bf16)] * count,
        compiler_params=pltpu.CompilerParams(vmem_limit_bytes=VMEM),
        cost_estimate=pl.CostEstimate(
            flops=3 * height * sum(widths) * count,
            bytes_accessed=14 * height * sum(widths) * count,
            transcendentals=0,
        ),
    )(place.reshape(1).astype(jnp.int32), *teachers, *students)
    return results[: len(teachers)], results[len(teachers) :]


def normalize_kernel(planes, core_ref, choose_ref, landed_ref, gain_ref, raw_ref, normed_ref):
    sources, blocks, slots, width = landed_ref.shape
    plane = normed_ref.shape[2]
    half = plane // CORES
    square = None
    for block in range(blocks):
        rows = landed_ref[:, block].astype(f32).reshape(sources * slots, width).astype(bf16)
        values = jnp.dot(choose_ref[...], rows, preferred_element_type=f32)
        raw_ref[block] = values.astype(bf16)
        part = jnp.sum(values * values, axis=1, keepdims=True)
        square = part if square is None else square + part
    scale = lax.rsqrt(square / (blocks * width) + norm_epsilon)
    core = core_ref[0]
    for first in range(0, blocks * width, half):
        block, start = first // width, first % width
        at = first // plane
        values = raw_ref[block, :, start : start + half].astype(f32)
        values = (values * scale * gain_ref[:, first : first + half]).astype(bf16)
        side = jnp.bitwise_xor(first % plane // half, core) * half
        normed_ref[at, :, pl.ds(pl.multiple_of(side, half), half)] = values


def normalize(choose, landed, gain, core_at, planes):
    rows = choose.shape[0]
    _, blocks, _, width = landed.shape
    return pl.pallas_call(
        functools.partial(normalize_kernel, planes),
        in_specs=[pl.BlockSpec(memory_space=pltpu.SMEM)]
        + [pl.BlockSpec(memory_space=pltpu.VMEM)] * 3,
        out_specs=[pl.BlockSpec(memory_space=pltpu.VMEM)] * 2,
        out_shape=[
            jax.ShapeDtypeStruct((blocks, rows, width), bf16),
            jax.ShapeDtypeStruct((planes, rows, blocks * width // planes), bf16),
        ],
        compiler_params=pltpu.CompilerParams(vmem_limit_bytes=VMEM),
        cost_estimate=pl.CostEstimate(
            flops=2 * rows * landed.size, bytes_accessed=4 * landed.size, transcendentals=0
        ),
    )(core_at.reshape(1).astype(jnp.int32), choose, landed, gain.reshape(1, -1))


def place_kernel(count, turned, place_ref, *refs):
    out_ref = refs[-1]
    height = refs[0].shape[0]
    for bits in range(count):
        at = jnp.bitwise_xor(place_ref[0], bits) * height
        at = pl.ds(pl.multiple_of(at, height), height)
        if turned:
            out_ref[:, at] = refs[bits][...].T
        else:
            out_ref[at, :] = refs[bits][...]


def in_order(by_bits, place, turned=False):
    count = len(by_bits)
    height, width = by_bits[0].shape
    shape = (width, count * height) if turned else (count * height, width)
    if turned and height % HEAD_WIDTH != 0:
        rows = [
            lax.dynamic_index_in_dim(
                jnp.stack(by_bits), jnp.bitwise_xor(place, i), 0, keepdims=False
            )
            for i in range(count)
        ]
        return jnp.concatenate(rows, axis=0).T
    return pl.pallas_call(
        functools.partial(place_kernel, count, turned),
        in_specs=[pl.BlockSpec(memory_space=pltpu.SMEM)]
        + [pl.BlockSpec(memory_space=pltpu.VMEM)] * count,
        out_specs=pl.BlockSpec(memory_space=pltpu.VMEM),
        out_shape=jax.ShapeDtypeStruct(shape, bf16),
        compiler_params=pltpu.CompilerParams(vmem_limit_bytes=VMEM),
        cost_estimate=pl.CostEstimate(
            flops=0, bytes_accessed=4 * count * height * width, transcendentals=0
        ),
    )(place.reshape(1).astype(jnp.int32), *by_bits)


def multiply_kernel(parts, *refs):
    rows, (mine_ref, other_ref, out_ref, all_ref) = refs[:parts], refs[parts:]
    height = rows[0].shape[0]
    depth = mine_ref.shape[0]

    @pl.when(pl.program_id(0) == 0)
    def _():
        for i, part in enumerate(rows):
            all_ref[i * height : (i + 1) * height, :] = part[...]

    product = jnp.dot(all_ref[:, :depth], mine_ref[...], preferred_element_type=f32)
    product += jnp.dot(all_ref[:, depth:], other_ref[...], preferred_element_type=f32)
    out_ref[...] = product.astype(out_ref.dtype)


def multiply(parts, mine, other, kind):
    height, depth = parts[0].shape
    width = mine.shape[1]
    tile = 512 if width % 512 == 0 else 128
    rows = pl.BlockSpec((height, depth), lambda i: (0, 0))
    weights = pl.BlockSpec((depth // CORES, tile), lambda i: (0, i))
    count = len(parts)
    return pl.pallas_call(
        functools.partial(multiply_kernel, count),
        grid=(width // tile,),
        in_specs=[rows] * count + [weights] * 2,
        out_specs=pl.BlockSpec((count * height, tile), lambda i: (0, i)),
        out_shape=jax.ShapeDtypeStruct((count * height, width), kind),
        scratch_shapes=[pltpu.VMEM((count * height, depth), bf16)],
        compiler_params=pltpu.CompilerParams(vmem_limit_bytes=24 * 1024 * 1024),
        cost_estimate=pl.CostEstimate(
            flops=2 * count * height * depth * width,
            bytes_accessed=2 * depth * width,
            transcendentals=0,
        ),
    )(*parts, mine, other)


def finish_kernel(
    turned_blocks, query_blocks, own_ref, up_ref, down_ref, cosine_ref, sine_ref, back_ref,
    query_ref, fresh_ref,
):
    wide = own_ref.shape[1] // HEAD_WIDTH
    first = pl.program_id(0) * wide
    values = own_ref[...] + up_ref[...].astype(f32) + down_ref[...].astype(f32)
    pieces = []
    for head in range(wide):
        piece = values[:, head * HEAD_WIDTH : (head + 1) * HEAD_WIDTH]
        rolled = pltpu.roll(piece, HEAD_WIDTH // 2, 1)
        turned = piece * cosine_ref[...] + rolled * sine_ref[...]
        pieces.append(jnp.where(first + head < turned_blocks, turned, piece).astype(bf16))
    values = jnp.concatenate(pieces, axis=1)
    values = jnp.dot(back_ref[...], values, preferred_element_type=f32).astype(bf16)

    @pl.when(first < query_blocks)
    def _():
        for head in range(wide):
            query_ref[head] = values[:, head * HEAD_WIDTH : (head + 1) * HEAD_WIDTH]

    @pl.when(first >= query_blocks)
    def _():
        fresh_ref[...] = values


def finish_projection(own, up, down, cosine_table, sine_table, back, query_blocks, key_blocks):
    tokens, width = own.shape
    blocks = width // HEAD_WIDTH
    wide = max(w for w in (1, 2, 4) if query_blocks % w == 0 and (blocks - query_blocks) % w == 0)
    column = pl.BlockSpec((tokens, wide * HEAD_WIDTH), lambda i: (0, i))
    table = pl.BlockSpec((tokens, HEAD_WIDTH), lambda i: (0, 0))
    steps = query_blocks // wide
    return pl.pallas_call(
        functools.partial(finish_kernel, query_blocks + key_blocks, query_blocks),
        grid=(blocks // wide,),
        in_specs=[column, column, column, table, table]
        + [pl.BlockSpec((tokens, tokens), lambda i: (0, 0))],
        out_specs=[
            pl.BlockSpec((wide, tokens, HEAD_WIDTH), lambda i: (jnp.minimum(i, steps - 1), 0, 0)),
            pl.BlockSpec((tokens, wide * HEAD_WIDTH), lambda i: (0, jnp.maximum(i - steps, 0))),
        ],
        out_shape=[
            jax.ShapeDtypeStruct((query_blocks, tokens, HEAD_WIDTH), bf16),
            jax.ShapeDtypeStruct((tokens, (blocks - query_blocks) * HEAD_WIDTH), bf16),
        ],
        compiler_params=pltpu.CompilerParams(vmem_limit_bytes=VMEM),
        cost_estimate=pl.CostEstimate(
            flops=2 * tokens * tokens * width,
            bytes_accessed=10 * tokens * width,
            transcendentals=0,
        ),
    )(own, up, down, cosine_table, sine_table, back)


def attend_kernel(rows, groups, lengths_ref, q_ref, fresh_ref, k_ref, v_ref, out_ref, total_ref):
    first = pl.program_id(0) * rows
    heads = q_ref.shape[0]
    slots, width = k_ref.shape[1], k_ref.shape[2]
    steps = DECODE_STEPS
    pair = 2 * steps
    height = heads * pair
    scale = HEAD_WIDTH ** (-0.5)
    contract_last = (((1,), (1,)), ((), ()))
    contract_mid = (((1,), (0,)), ((), ()))
    fresh_k = fresh_ref[:, :width]
    fresh_v = fresh_ref[:, width:]
    pairs = rows // 2
    queries = q_ref[...].astype(f32)
    band = height // groups
    wide = []
    for p in range(pairs):
        query = queries[:, p * pair : (p + 1) * pair, :].reshape(height, HEAD_WIDTH)
        if groups > 1:
            row_band = lax.broadcasted_iota(jnp.int32, (height, HEAD_WIDTH), 0) // band
            query = jnp.concatenate(
                [jnp.where(row_band == g, query, 0.0) for g in range(groups)], axis=1
            )
        wide.append(query.astype(bf16))
    second = (lax.broadcasted_iota(jnp.int32, (height, 1), 0) % pair) >= steps
    slot_index = lax.broadcasted_iota(jnp.int32, (height, slots), 1)
    fresh_index = lax.broadcasted_iota(jnp.int32, (height, rows * steps), 1)
    token_of = lax.broadcasted_iota(jnp.int32, (height, rows * steps), 0) % pair
    cached_scores, fresh_scores = [], []
    for p in range(pairs):
        one = lax.dot_general(wide[p], k_ref[2 * p], contract_last, preferred_element_type=f32)
        two = lax.dot_general(wide[p], k_ref[2 * p + 1], contract_last, preferred_element_type=f32)
        length = jnp.where(
            second, lengths_ref[first + 2 * p + 1], lengths_ref[first + 2 * p]
        )
        scores = jnp.where(second, two, one) * scale
        cached_scores.append(jnp.where(slot_index < length, scores, masked_score))
        fresh = lax.dot_general(wide[p], fresh_k, contract_last, preferred_element_type=f32)
        token = token_of + p * pair
        valid = (fresh_index // steps == token // steps) & (fresh_index <= token)
        fresh_scores.append(jnp.where(valid, fresh * scale, masked_score))
    for p in range(pairs):
        cached, fresh = cached_scores[p], fresh_scores[p]
        highest = jnp.maximum(
            jnp.max(cached, axis=-1, keepdims=True), jnp.max(fresh, axis=-1, keepdims=True)
        )
        cached = jnp.exp(cached - highest)
        fresh = jnp.exp(fresh - highest)
        totals = jnp.sum(cached, axis=-1, keepdims=True) + jnp.sum(fresh, axis=-1, keepdims=True)
        cached = cached / totals
        fresh = (fresh / totals).astype(bf16)
        attended = lax.dot_general(
            jnp.where(second, 0.0, cached).astype(bf16),
            v_ref[2 * p],
            contract_mid,
            preferred_element_type=f32,
        )
        attended += lax.dot_general(
            jnp.where(second, cached, 0.0).astype(bf16),
            v_ref[2 * p + 1],
            contract_mid,
            preferred_element_type=f32,
        )
        attended += lax.dot_general(fresh, fresh_v, contract_mid, preferred_element_type=f32)
        for head in range(heads):
            group = head * groups // heads
            total_ref[p * pair : (p + 1) * pair, head * HEAD_WIDTH : (head + 1) * HEAD_WIDTH] = (
                attended[
                    head * pair : (head + 1) * pair,
                    group * HEAD_WIDTH : (group + 1) * HEAD_WIDTH,
                ]
            )
    out_ref[...] = total_ref[...].astype(bf16)


def attend(queries, fresh, key_cache, value_cache, lengths):
    heads, tokens = queries.shape[0], queries.shape[1]
    row_count, slots, width = key_cache.shape
    groups = width // HEAD_WIDTH
    rows = 8
    held = rows * DECODE_STEPS
    return pl.pallas_call(
        functools.partial(attend_kernel, rows, groups),
        grid=(row_count // rows,),
        in_specs=[
            pl.BlockSpec(memory_space=pltpu.SMEM),
            pl.BlockSpec((heads, held, HEAD_WIDTH), lambda i: (0, i, 0)),
            pl.BlockSpec((held, 2 * width), lambda i: (i, 0)),
            pl.BlockSpec((rows, slots, width), lambda i: (i, 0, 0)),
            pl.BlockSpec((rows, slots, width), lambda i: (i, 0, 0)),
        ],
        out_specs=pl.BlockSpec((held, heads * HEAD_WIDTH), lambda i: (i, 0)),
        out_shape=jax.ShapeDtypeStruct((tokens, heads * HEAD_WIDTH), bf16),
        scratch_shapes=[pltpu.VMEM((held, heads * HEAD_WIDTH), f32)],
        compiler_params=pltpu.CompilerParams(vmem_limit_bytes=VMEM),
        cost_estimate=pl.CostEstimate(
            flops=8 * tokens * heads * slots * width,
            bytes_accessed=4 * row_count * slots * width,
            transcendentals=tokens * heads * slots,
        ),
    )(lengths, queries, fresh, key_cache, value_cache)


def term_kernel(places, info_ref, own_ref, other_ref, *refs):
    blocks = refs[: len(places)]
    own_out_ref, other_out_ref, weights_ref, arrival = refs[len(places) :]
    for place, block in zip(places, blocks):

        @pl.when(info_ref[0] == place)
        def _(block=block):
            copy = pltpu.make_async_copy(block, weights_ref, arrival)
            copy.start()
            copy.wait()

    weights = weights_ref[...]
    for rows_ref, out_ref in ((own_ref, own_out_ref), (other_ref, other_out_ref)):
        product = jnp.dot(rows_ref[...], weights, preferred_element_type=f32)
        out_ref[...] = product.astype(out_ref.dtype)


def term(own, other, blocks, place, own_type, other_type):
    places = sorted(blocks)
    depth, height = blocks[0].shape
    tokens = own.shape[0]
    whole = pl.BlockSpec(memory_space=pltpu.VMEM)
    return pl.pallas_call(
        functools.partial(term_kernel, places),
        in_specs=[pl.BlockSpec(memory_space=pltpu.SMEM), whole, whole]
        + [pl.BlockSpec(memory_space=pl.ANY)] * len(places),
        out_specs=[whole, whole],
        out_shape=[
            jax.ShapeDtypeStruct((tokens, height), own_type),
            jax.ShapeDtypeStruct((tokens, height), other_type),
        ],
        scratch_shapes=[pltpu.VMEM((depth, height), bf16), pltpu.SemaphoreType.DMA],
        compiler_params=pltpu.CompilerParams(vmem_limit_bytes=VMEM),
        cost_estimate=pl.CostEstimate(
            flops=4 * tokens * height * depth,
            bytes_accessed=2 * height * depth + 12 * tokens * height,
            transcendentals=0,
        ),
    )(place.reshape(1).astype(jnp.int32), own, other, *[blocks[p] for p in places])


def sum_over_tensor(attended, blocks, t_at, z_at, core_at, count):
    other = lax.ppermute(attended, "core", [(0, 1), (1, 0)])

    def of(bits, own_type, other_type):
        place = jnp.bitwise_xor(t_at, bits) - z_at
        return term(attended, other, blocks, place, own_type, other_type)

    if count == 4:
        far_own, far_other = of(3, bf16, bf16)
        far_own, far_other = swap(far_own, 1, count), swap(far_other, 2, count)
        near_own, pass_other = of(1, bf16, f32)
        near_own = swap(near_own, 1, count)
        pass_own, near_other = of(2, f32, bf16)
        near_other = swap(near_other, 2, count)
        pass_other = swap((pass_other + far_other.astype(f32)).astype(bf16), 1, count)
        pass_own = swap((pass_own + far_own.astype(f32)).astype(bf16), 2, count)
        sum_own, sum_other = of(0, f32, f32)
        sum_other = sum_other + near_other.astype(f32) + pass_other.astype(f32)
        sum_own = sum_own + near_own.astype(f32) + pass_own.astype(f32)
    else:
        terms = [
            term(attended, other, blocks, jnp.int32(b) - z_at, bf16, bf16) for b in range(count)
        ]
        sum_own, sum_other = (
            lax.psum_scatter(
                jnp.concatenate(rows, axis=1), "tensor", scatter_dimension=1, tiled=True
            ).astype(f32)
            for rows in zip(*terms)
        )
    came = lax.ppermute(sum_other.astype(bf16), "core", [(0, 1), (1, 0)]).astype(f32)
    return jnp.where(
        core_at == 0,
        jnp.concatenate([sum_own, came], axis=1),
        jnp.concatenate([came, sum_own], axis=1),
    )


def body(
    n_z,
    n_t,
    token_ids,
    cache_lengths,
    embedding,
    norm_gain,
    rotated_key_cache,
    stored_value_cache,
    teacher_q,
    teacher_k,
    teacher_v,
    teacher_o,
    student_q,
    student_k,
    student_v,
    student_o,
):
    n_r = n_z * CORES
    z_at, core_at, t_at = (lax.axis_index(name) for name in ("z", "core", "tensor"))
    rows, steps = token_ids.shape
    tokens = rows * steps
    shard_rows, feature_block = embedding.shape
    capacity = 2 * tokens // n_r
    quarter_slots = capacity // n_t
    quarter = tokens // n_t

    ids = token_ids.reshape(tokens)
    owner = ids // shard_rows
    is_owner = (owner[:, None] == jnp.arange(n_r)[None, :]).astype(jnp.int32)
    before = jnp.cumsum(is_owner, axis=0) - is_owner
    rank = jnp.sum(before * is_owner, axis=1)
    counts = jnp.sum(is_owner, axis=0)
    starts = jnp.cumsum(counts) - counts
    place = jnp.sum(is_owner * starts[None, :], axis=1) + rank
    part, spot = place % n_t, place // n_t
    slot = rank // n_t
    request_at = (owner * n_t + part) * quarter_slots + slot
    wanted = jnp.sum(
        jnp.where(
            request_at[None, :] == jnp.arange(n_r * capacity)[:, None],
            (ids - owner * shard_rows)[None, :],
            0,
        ),
        axis=1,
    ).reshape(n_r, capacity)
    asked = lax.all_to_all(wanted, ("z", "core"), 0, 0, tiled=True)

    (next_q, next_k, next_v), qkv_columns = blend(
        (teacher_q, teacher_k, teacher_v), (student_q, student_k, student_v), t_at, n_t
    )
    (next_o,), o_columns = blend((teacher_o,), (student_o,), t_at, n_t)
    qkv_by_bits = [x if b == 0 else swap(x, b, n_t) for b, x in enumerate(qkv_columns)]

    weights = in_order(qkv_by_bits, t_at)
    other = lax.ppermute(weights, "core", [(0, 1), (1, 0)])

    asked = after(asked, qkv_columns[-1])
    picked = jnp.take(embedding, asked.reshape(-1), axis=0, mode="clip")
    picked = picked.reshape(n_r * n_t, quarter_slots, feature_block)
    landed = lax.all_to_all(picked, ("z", "core", "tensor"), 0, 0, tiled=True)
    mine = (part == t_at)[None, :] & (spot[None, :] == jnp.arange(quarter)[:, None])
    source = jnp.sum(jnp.where(mine, (owner * quarter_slots + slot)[None, :], 0), axis=1)
    choose = (source[:, None] == jnp.arange(n_r * quarter_slots)[None, :]).astype(bf16)
    landed = landed.reshape(n_r, n_t, quarter_slots, feature_block)
    for columns in qkv_by_bits[1:]:
        choose = after(choose, columns)
    raw, normed = normalize(choose, landed, norm_gain, core_at, n_z)
    held = lax.all_to_all(normed, "z", 0, 0, tiled=True)

    o_by_bits = [
        x if b == 0 else swap(after(x, normed), b, n_t) for b, x in enumerate(o_columns)
    ]
    rows_o = in_order(o_by_bits, t_at, turned=True)

    order = jnp.asarray(due_order(n_z))[z_at]
    products = []
    for k in range(n_z):
        chunk = lax.dynamic_index_in_dim(held, order[k], 0, keepdims=False)
        if k == 0:
            for columns in o_by_bits[1:]:
                chunk = after(chunk, columns)
        chunk = [chunk] + [swap(chunk, b, n_t) for b in range(1, n_t)]
        last = chunk[-1]
        products.append(multiply(chunk, weights, other, f32 if k == n_z - 1 else bf16))
    blocks_o = line_gather(after(rows_o, held), n_z)
    gates = [blocks_o[-step] for step in range(1, n_z)]
    own, up, down = line_sum(products, z_at, n_z, gates)

    raw = after(raw, last)
    raw_by_bits = []
    for b in range(n_t):
        block = lax.dynamic_index_in_dim(raw, jnp.bitwise_xor(t_at, b), 0, keepdims=False)
        raw_by_bits.append(block if b == 0 else swap(block, b, n_t))
    residual = jnp.concatenate(raw_by_bits, axis=0)

    column = jnp.bitwise_xor(part, t_at) * quarter + spot
    back = column[:, None] == jnp.arange(tokens)[None, :]
    positions = (cache_lengths[:, None] + jnp.arange(steps, dtype=jnp.int32)[None, :]).reshape(-1)
    moved = jnp.sum(jnp.where(back, positions[:, None], 0), axis=0).astype(f32)
    inverse = rope_theta ** (-(jnp.arange(HEAD_WIDTH // 2, dtype=f32) * 2.0) / HEAD_WIDTH)
    angles = moved[:, None] * inverse
    cosine_table, sine_table = jnp.cos(angles), jnp.sin(angles)
    cosine_table = jnp.concatenate([cosine_table, cosine_table], axis=1)
    sine_table = jnp.concatenate([-sine_table, sine_table], axis=1)
    back = after(after(back.astype(bf16), blocks_o[1 - n_z]), blocks_o[n_z - 1])
    residual = jnp.dot(back, residual, preferred_element_type=f32)

    q_width = teacher_q.shape[1] // n_t
    k_width = teacher_k.shape[1] // n_t
    queries, fresh = finish_projection(
        own,
        up,
        down,
        cosine_table,
        sine_table,
        back,
        q_width // HEAD_WIDTH,
        k_width // HEAD_WIDTH,
    )
    attended = attend(queries, fresh, rotated_key_cache, stored_value_cache, cache_lengths)

    hidden = residual + sum_over_tensor(
        attended, blocks_o, t_at, z_at, core_at, n_t
    )
    hidden_out = hidden.astype(bf16).reshape(rows, steps, feature_block)
    return (next_q, next_k, next_v, next_o, hidden_out)


def solution(mesh):
    n_z = mesh.shape["replica"] // CORES
    n_t = mesh.shape["tensor"]
    split = jax.sharding.Mesh(mesh.devices.reshape(n_z, CORES, n_t), ("z", "core", "tensor"))
    replica = ("z", "core")
    every = ("z", "core", "tensor")
    return jax.shard_map(
        functools.partial(body, n_z, n_t),
        mesh=split,
        in_specs=(
            P(replica, None),
            P(replica),
            P(replica, "tensor"),
            P(),
            P(replica, None, "tensor"),
            P(replica, None, "tensor"),
        )
        + (P(every, None),) * 8,
        out_specs=(P(every, None),) * 4 + (P(replica, None, "tensor"),),
        check_vma=False,
    )
```

time: 966 us -> 461 us (0.48)
  waiting for transfers between devices: 529 us -> 206 us
  matrix products: 165 us -> 2.24 us
  Pallas kernels: 0 us -> 89.6 us
  starting transfers between devices: 1.26 us -> 89.9 us
  blocking collectives: 81 us -> 0 us
  local copies, waits for them, and re-layouts: 109 us -> 39.6 us
  other arithmetic: 54.1 us -> 23.3 us
    all_gather x8 -> x0, waiting for transfers between devices: 372 us -> none  [the longest x1 140 us: body(): lax.all_gather(moved[0], 'replica', axis=0, tiled=True)]
    ppermute x0 -> x41, waiting for transfers between devices: none -> 206 us  [the longest x27 184 us: swap(): return lax.ppermute(values, 'tensor', [(i, i ^ bits) for i in range(count)])]
    dot_general x31 -> x1, matrix products: 165 us -> 2.24 us  [body(): residual = jnp.dot(back, residual, preferred_element_type=f32)]
    reduce_scatter x5 -> x0, waiting for transfers between devices: 155 us -> none  [the longest x1 129 us: body(): lax.psum_scatter(terms.astype(jnp.bfloat16), 'replica', scatter_dimension...]
    pallas_call x0 -> x31, Pallas kernels: none -> 89.6 us  [the longest x4 23.1 us: term(): pl.pallas_call(functools.partial(term_kernel, places), in_specs=[pl.Block...]
    ppermute x0 -> x41, starting transfers between devices: none -> 72.8 us  [the longest x27 28.6 us: swap(): return lax.ppermute(values, 'tensor', [(i, i ^ bits) for i in range(count)])]
    all_to_all x4 -> x0, blocking collectives: 66.5 us -> none  [the longest x1 21.8 us: body(): lax.all_to_all(low_blocks[3], 'tensor', split_axis=1, concat_axis=0, tile...]
    gather x2 -> x1, local copies, waits for them, and re-layouts: 50.6 us -> 14.9 us  [body(): picked = jnp.take(embedding, asked.reshape(-1), axis=0, mode='clip')]
  transfers between devices with their start and end apart: 13 -> 44, of which waited for: 7 -> 24; matrix products, arithmetic and copies ran while one was open for 25% -> 6% of each run, Pallas kernels for 0% -> 13%
where the time goes in v1:
time: 461 us; the launch traced here: 459 us
  waiting for transfers between devices  206 us (45%)
  starting transfers between devices  89.9 us (20%)
  Pallas kernels  89.6 us (19%)
  local copies, waits for them, and re-layouts  39.6 us (9%)
  other arithmetic  23.3 us (5%)
  between operations  8.48 us (2%)
    ppermute x27, waiting for transfers between devices, swap(): return lax.ppermute(values, 'tensor', [(i, i ^ bits) for i in range(count)])  184 us
    ppermute x27, starting transfers between devices, swap(): return lax.ppermute(values, 'tensor', [(i, i ^ bits) for i in range(count)])  28.6 us
    pallas_call x4, Pallas kernels, term(): pl.pallas_call(functools.partial(term_kernel, places), in_specs=[pl.Block...  23.1 us
    pallas_call x4, Pallas kernels, multiply(): pl.pallas_call(functools.partial(multiply_kernel, count), grid=(width //...  19.5 us
    ppermute x1, waiting for transfers between devices, line_sum(): down = lax.ppermute(block, 'z', [(3, 2), (2, 1), (1, 0)])  18.5 us
    ppermute x1, starting transfers between devices, line_sum(): up = lax.ppermute(block, 'z', [(0, 1), (1, 2), (2, 3)])  18.3 us
    pallas_call x2, Pallas kernels, blend(): pl.pallas_call(functools.partial(blend_kernel, widths), grid_spec=pltpu.P...  15.6 us
    gather x1, local copies, waits for them, and re-layouts, body(): picked = jnp.take(embedding, asked.reshape(-1), axis=0, mode='clip')  14.9 us
  transfers between devices with their start and end apart: 44, of which 24 were waited for; matrix products, arithmetic and copies ran while one was open for 6% of the time, Pallas kernels for 13%

profile of v1, /device:TPU:0, one launch (start us, length us, event | category | flops | bytes accessed | tf_op | source)
XLA Modules:
  0.0 459.0 jit_solution(858829027059142527)
XLA Ops:
  5.9 6.3 %all-to-all-start = ((s32[8,1,96]{2,1,0:T(1,128)}), s32[8,1,96]{2,1,0:T(1,128)S(1)}, u32[]{:S(2)}, u32[]{:S(2)}) async-start(s32[8,1,96]{2,1,0:T(1,128)} %all_to_all.13), calls=%async_computation | async-start | bytes 8192 | tf_op jit(solution)/shard_map/all_to_all | solution.py:547
  12.2 8.8 %shard_map.182 = (f32[256,4096]{1,0:T(8,128)}, f32[256,1024]{1,0:T(8,128)}, f32[256,1024]{1,0:T(8,128)}, bf16[256,1536]{1,0:T(8,128)(2,1)}, bf16[256,1536]{1,0:T...) custom-call(s32[1]{0:T(128)} %bitcast.place_ref, f32[256,4096]{1,0:T(8,128)} %refs_0_.2, ...), custom_call_target="tpu_custom_call" | custom-call | flops 4718592 | bytes 22020096 | tf_op jit(solution)/shard_map/pallas_call | solution.py:129
  22.3 14.9 %gather_fusion = bf16[768,2048]{1,0:T(8,128)(2,1)} fusion(bf16[4008,2048]{1,0:T(8,128)(2,1)} %param.17, s32[1024]{0:T(1024)S(1)} %pad_clamp_fusion), kind=kCustom, calls=%fused_computation | custom fusion | bytes 6294528 | tf_op jit(solution)/shard_map/jit(_take)/gather | solution.py:559
  37.2 6.1 %all-to-all-start.1 = ((bf16[32,24,2048]{2,1,0:T(8,128)(2,1)}), bf16[32,24,2048]{2,1,0:T(8,128)(2,1)S(1)}, u32[]{:S(2)}, u32[]{:S(2)}) async-start(bf16[32,24,2048]{2,1,0:T(8,128)(2,1)} %bitcast.40), calls=%async_computation.1 | async-start | bytes 6291456 | tf_op jit(solution)/shard_map/all_to_all | solution.py:561
  43.3 1.8 collective-permute-start
  45.1 1.5 collective-permute-start.1
  47.7 44.4 %collective-permute-done.other_ref.refs_1_ = bf16[256,1536]{1,0:T(8,128)(2,1)} collective-permute-done((bf16[256,1536]{1,0:T(8,128)(2,1)}, bf16[256,1536]{1,0:T(8,128)(2,1)}, u32[]{:S(2)}, u32[]{:S(2)}) %collective-permute-start) | collective-permute-done | bytes 786464 | tf_op jit(solution)/shard_map/ppermute | solution.py:28
  93.1 23.3 %collective-permute-done.2.other_ref.refs_3_ = bf16[256,1536]{1,0:T(8,128)(2,1)} collective-permute-done((bf16[256,1536]{1,0:T(8,128)(2,1)}, bf16[256,1536]{1,0:T(8,128)(2,1)}, u32[]{:S(2)}, u32[]{:S(2)}) %collective-permute-start.2) | collective-permute-done | bytes 786464 | tf_op jit(solution)/shard_map/ppermute | solution.py:28
  116.4 1.7 copy-done.14
  118.0 4.5 shard_map.188
  122.5 4.7 %all-to-all-start.2 = ((bf16[4,96,2048]{2,1,0:T(8,128)(2,1)}), bf16[4,96,2048]{2,1,0:T(8,128)(2,1)S(1)}, u32[]{:S(2)}, u32[]{:S(2)}) async-start(bf16[4,96,2048]{2,1,0:T(8,128)(2,1)} %get-tuple-element.38.other_ref), calls=%async_computation.2 | async-start | bytes 3145728 | tf_op jit(solution)/shard_map/all_to_all | solution.py:569
  127.2 3.7 shard_map.197.refs_4_
  130.9 6.8 %shard_map.183 = (f32[256,4096]{1,0:T(8,128)}, bf16[256,1024]{1,0:T(8,128)(2,1)}, bf16[256,1024]{1,0:T(8,128)(2,1)}, bf16[256,1024]{1,0:T(8,128)(2,1)}, bf16[256,1024]{1,0:T(8,128)(2,1)}) custom-call(s32[1]{0:T(128)} %bitcast.place_ref, f32[256,4096]{1,0:T(8,128)} %refs_0_.3, f32[256,4096]{1,0:T(8,128)} %refs_1_.3), custom_call_target="tpu_custom_call" | custom-call | flops 3145728 | bytes 14680064 | tf_op jit(solution)/shard_map/pallas_call | solution.py:129
  137.7 2.8 collective-permute-start.3
  140.5 1.5 collective-permute-start.5
  142.1 11.4 %collective-permute-done.3.refs_1_.other_ref = bf16[256,1024]{1,0:T(8,128)(2,1)S(1)} collective-permute-done((bf16[256,1024]{1,0:T(8,128)(2,1)}, bf16[256,1024]{1,0:T(8,128)(2,1)S(1)}, u32[]{:S(2)}, u32[]{:S(2)}) %collective-permute-start.3) | collective-permute-done | bytes 524320 | tf_op jit(solution)/shard_map/ppermute | solution.py:28
  153.5 12.5 %collective-permute-done.4.refs_2_.other_ref = bf16[256,1024]{1,0:T(8,128)(2,1)S(1)} collective-permute-done((bf16[256,1024]{1,0:T(8,128)(2,1)}, bf16[256,1024]{1,0:T(8,128)(2,1)S(1)}, u32[]{:S(2)}, u32[]{:S(2)}) %collective-permute-start.4) | collective-permute-done | bytes 524320 | tf_op jit(solution)/shard_map/ppermute | solution.py:28
  167.1 3.5 shard_map.192.values_ref
  171.7 5.3 %collective-permute-start.6 = (bf16[1024,1024]{1,0:T(8,128)(2,1)}, bf16[1024,1024]{1,0:T(8,128)(2,1)}, u32[]{:S(2)}, u32[]{:S(2)}) collective-permute-start(bf16[1024,1024]{1,0:T(8,128)(2,1)} %shard_map.193.refs_3_), channel_id=1, source_target_pairs={{0,8},{8,16},{16,24},{1,9},{9,17},{17,25},{2,10},{10,18},{18,26},{... | collective-permute-start | bytes 6291464 | tf_op jit(solution)/shard_map/ppermute | solution.py:97
  187.1 2.4 dynamic-slice_bitcast_fusion.1
  191.2 1.9 collective-permute-start.21
  193.1 8.8 %collective-permute-done.19.refs_1_ = bf16[96,2048]{1,0:T(8,128)(2,1)S(1)} collective-permute-done((bf16[96,2048]{1,0:T(8,128)(2,1)}, bf16[96,2048]{1,0:T(8,128)(2,1)S(1)}, u32[]{:S(2)}, u32[]{:S(2)}) %collective-permute-start.19) | collective-permute-done | bytes 393248 | tf_op jit(solution)/shard_map/ppermute | solution.py:28
  201.9 6.9 %collective-permute-done.20.refs_2_ = bf16[96,2048]{1,0:T(8,128)(2,1)S(1)} collective-permute-done((bf16[96,2048]{1,0:T(8,128)(2,1)}, bf16[96,2048]{1,0:T(8,128)(2,1)S(1)}, u32[]{:S(2)}, u32[]{:S(2)}) %collective-permute-start.20) | collective-permute-done | bytes 393248 | tf_op jit(solution)/shard_map/ppermute | solution.py:28
  209.8 4.7 %shard_map.202 = bf16[384,1536]{1,0:T(8,128)(2,1)S(1)} custom-call(bf16[96,2048]{1,0:T(8,128)(2,1)S(1)} %copy-done.1, bf16[96,2048]{1,0:T(8,128)(2,1)S(1)} %collective-permute-done.19.refs_1_, bf16[96,2048]{1,0:T(8,128)(2,1)S(1)} %collective-permute-done.20.refs_2_, bf16[96,2048]{1,0:T(8,128)(2,1)S(1)} %collective-permute-done.21.refs_3_, ...), custom_call_target="tpu_custom_call" | custom-call | flops 2415919104 | bytes 6291456 | tf_op jit(solution)/shard_map/pallas_call | solution.py:249
  214.6 5.3 %collective-permute-start.28 = (bf16[384,1536]{1,0:T(8,128)(2,1)S(1)}, bf16[384,1536]{1,0:T(8,128)(2,1)}, u32[]{:S(2)}, u32[]{:S(2)}) collective-permute-start(bf16[384,1536]{1,0:T(8,128)(2,1)S(1)} %shard_map.202), channel_id=1, source_target_pairs={{0,8},{24,16},{1,9},{25,17},{2,10},{26,18},{3,11},{27,19},{4,12},{... | collective-permute-start | bytes 3538952 | tf_op jit(solution)/shard_map/ppermute | solution.py:60
  221.6 6.5 %collective-permute-done.25.refs_1_ = bf16[96,2048]{1,0:T(8,128)(2,1)S(1)} collective-permute-done((bf16[96,2048]{1,0:T(8,128)(2,1)S(1)}, bf16[96,2048]{1,0:T(8,128)(2,1)S(1)}, u32[]{:S(2)}, u32[]{:S(2)}) %collective-permute-start.25) | collective-permute-done | bytes 393248 | tf_op jit(solution)/shard_map/ppermute | solution.py:28
  228.1 1.9 collective-permute-start.27
  230.0 2.0 collective-permute-start.7
  232.0 1.5 collective-permute-start.10
  235.6 5.4 %collective-permute-done.27.refs_3_ = bf16[96,2048]{1,0:T(8,128)(2,1)S(1)} collective-permute-done((bf16[96,2048]{1,0:T(8,128)(2,1)S(1)}, bf16[96,2048]{1,0:T(8,128)(2,1)S(1)}, u32[]{:S(2)}, u32[]{:S(2)}) %collective-permute-start.27) | collective-permute-done | bytes 393248 | tf_op jit(solution)/shard_map/ppermute | solution.py:28
  241.0 4.7 %shard_map.204 = bf16[384,1536]{1,0:T(8,128)(2,1)S(1)} custom-call(bf16[96,2048]{1,0:T(8,128)(2,1)S(1)} %copy-done.9, bf16[96,2048]{1,0:T(8,128)(2,1)S(1)} %collective-permute-done.25.refs_1_, bf16[96,2048]{1,0:T(8,128)(2,1)S(1)} %collective-permute-done.26.refs_2_, bf16[96,2048]{1,0:T(8,128)(2,1)S(1)} %collective-permute-done.27.refs_3_, ...), custom_call_target="tpu_custom_call" | custom-call | flops 2415919104 | bytes 6291456 | tf_op jit(solution)/shard_map/pallas_call | solution.py:249
  246.8 2.9 add_convert_fusion.2
  249.7 4.4 collective-permute-start.29
  254.1 1.7 collective-permute-start.31
  256.1 9.0 %collective-permute-done.23.refs_2_ = bf16[96,2048]{1,0:T(8,128)(2,1)S(1)} collective-permute-done((bf16[96,2048]{1,0:T(8,128)(2,1)}, bf16[96,2048]{1,0:T(8,128)(2,1)S(1)}, u32[]{:S(2)}, u32[]{:S(2)}) %collective-permute-start.23) | collective-permute-done | bytes 393248 | tf_op jit(solution)/shard_map/ppermute | solution.py:28
  266.0 1.7 collective-permute-start.24
  267.6 8.1 %collective-permute-done.24.refs_3_ = bf16[96,2048]{1,0:T(8,128)(2,1)} collective-permute-done((bf16[96,2048]{1,0:T(8,128)(2,1)}, bf16[96,2048]{1,0:T(8,128)(2,1)}, u32[]{:S(2)}, u32[]{:S(2)}) %collective-permute-start.24) | collective-permute-done | bytes 393248 | tf_op jit(solution)/shard_map/ppermute | solution.py:28
  277.0 2.0 collective-permute-start.8
  281.2 5.0 %shard_map.203 = bf16[384,1536]{1,0:T(8,128)(2,1)S(1)} custom-call(bf16[96,2048]{1,0:T(8,128)(2,1)} %get-tuple-element.66.refs_0_, bf16[96,2048]{1,0:T(8,128)(2,1)} %collective-permute-done.22.refs_1_, bf16[96,2048]{1,0:T(8,128)(2,1)S(1)} %copy-done.11, bf16[96,2048]{1,0:T(8,128)(2,1)} %collective-permute-done.24.refs_3_, bf16[1024,1536]{1,0:T(8,128)(2,1)S(1)} %copy-done, ...), custom_call_target="tpu_custom_call" | custom-call | flops 2415919104 | bytes 6291456 | tf_op jit(solution)/shard_map/pallas_call | solution.py:249
  288.6 4.5 add_convert_fusion
  293.1 18.3 %collective-permute-start.30 = (bf16[384,1536]{1,0:T(8,128)(2,1)}, bf16[384,1536]{1,0:T(8,128)(2,1)}, u32[]{:S(2)}, u32[]{:S(2)}) collective-permute-start(bf16[384,1536]{1,0:T(8,128)(2,1)} %get-tuple-element.61), channel_id=1, source_target_pairs={{0,8},{8,16},{16,24},{1,9},{9,17},{17,25},{2,10},{10,18},{18,26},{... | collective-permute-start | bytes 3538952 | tf_op jit(solution)/shard_map/ppermute | solution.py:68
  317.4 6.0 %collective-permute-done.12.other_ref.refs_3_ = bf16[96,2048]{1,0:T(8,128)(2,1)S(1)} collective-permute-done((bf16[96,2048]{1,0:T(8,128)(2,1)}, bf16[96,2048]{1,0:T(8,128)(2,1)S(1)}, u32[]{:S(2)}, u32[]{:S(2)}) %collective-permute-start.12) | collective-permute-done | bytes 393248 | tf_op jit(solution)/shard_map/ppermute | solution.py:28
  324.4 5.0 %shard_map.198.own_ref = f32[384,1536]{1,0:T(8,128)S(1)} custom-call(bf16[96,2048]{1,0:T(8,128)(2,1)S(1)} %copy-done.8, bf16[96,2048]{1,0:T(8,128)(2,1)} %collective-permute-done.16.refs_1_, bf16[96,2048]{1,0:T(8,128)(2,1)} %collective-permute-done.17.refs_2_, bf16[96,2048]{1,0:T(8,128)(2,1)S(1)} %collective-permute-done.12.other_ref.refs_3_, ...), custom_call_target="tpu_custom_call" | custom-call | flops 2415919104 | bytes 6291456 | tf_op jit(solution)/shard_map/pallas_call | solution.py:249
  329.5 1.4 copy-done.2
  332.0 18.5 %collective-permute-done.32.down_ref = bf16[384,1536]{1,0:T(8,128)(2,1)} collective-permute-done((bf16[384,1536]{1,0:T(8,128)(2,1)}, bf16[384,1536]{1,0:T(8,128)(2,1)}, u32[]{:S(2)}, u32[]{:S(2)}) %collective-permute-start.32) | collective-permute-done | bytes 1179680 | tf_op jit(solution)/shard_map/ppermute | solution.py:71
  350.5 5.3 %shard_map.207 = (bf16[8,384,128]{2,1,0:T(8,128)(2,1)}, bf16[384,512]{1,0:T(8,128)(2,1)}) custom-call(f32[384,1536]{1,0:T(8,128)} %copy-done.2, bf16[384,1536]{1,0:T(8,128)(2,1)} %collective-permute-done.30.up_ref, bf16[384,1536]{1,0:T(8,128)(2,1)} %collective-permute-done.32.down_ref, f32[384,128]{1,0:T(8,128)} %get-tuple-element.79.cosine_ref, ...), custom_call_target="tpu_custom_call" | custom-call | flops 452984832 | bytes 5898240 | tf_op jit(solution)/shard_map/pallas_call | solution.py:298
  355.8 14.5 %shard_map.208.own_ref = bf16[384,1024]{1,0:T(8,128)(2,1)} custom-call(s32[96]{0:T(128)} %lengths_ref.1, bf16[8,384,128]{2,1,0:T(8,128)(2,1)} %get-tuple-element.43.q_ref, bf16[384,512]{1,0:T(8,128)(2,1)} %get-tuple-element.44.fresh_ref, bf16[96,160,256]{2,1,0:T(8,128)(2,1)} %k_ref.1, bf16[96,160,256]{2,1,0:T(8,128)(2,1)} %v_ref.1), custom_call_target="tpu_custom_call" | custom-call | flops 1006632960 | bytes 15728640 | tf_op jit(solution)/shard_map/pallas_call | solution.py:401
  370.3 2.5 collective-permute-done.33.other_ref
  373.7 5.6 %shard_map.212 = (bf16[384,1024]{1,0:T(8,128)(2,1)}, bf16[384,1024]{1,0:T(8,128)(2,1)}) custom-call(s32[1]{0:T(128)} %bitcast.25.info_ref, bf16[384,1024]{1,0:T(8,128)(2,1)} %shard_map.208.own_ref, bf16[384,1024]{1,0:T(8,128)(2,1)} %copy-done.13, bf16[1024,1024]{1,0:T(8,128)(2,1)} %collective-permute-done.8.other_ref.refs_0_, ...), custom_call_target="tpu_custom_call" | custom-call | flops 1610612736 | bytes 6815744 | tf_op jit(solution)/shard_map/pallas_call | solution.py:445
  380.9 5.7 %shard_map.211 = (f32[384,1024]{1,0:T(8,128)}, bf16[384,1024]{1,0:T(8,128)(2,1)}) custom-call(s32[1]{0:T(128)} %bitcast.24.info_ref, bf16[384,1024]{1,0:T(8,128)(2,1)} %shard_map.208.own_ref, bf16[384,1024]{1,0:T(8,128)(2,1)} %copy-done.13, bf16[1024,1024]{1,0:T(8,128)(2,1)} %collective-permute-done.8.other_ref.refs_0_, ...), custom_call_target="tpu_custom_call" | custom-call | flops 1610612736 | bytes 6815744 | tf_op jit(solution)/shard_map/pallas_call | solution.py:445
  387.4 5.9 %shard_map.210 = (bf16[384,1024]{1,0:T(8,128)(2,1)}, f32[384,1024]{1,0:T(8,128)}) custom-call(s32[1]{0:T(128)} %bitcast.23.info_ref, bf16[384,1024]{1,0:T(8,128)(2,1)} %shard_map.208.own_ref, bf16[384,1024]{1,0:T(8,128)(2,1)} %copy-done.13, bf16[1024,1024]{1,0:T(8,128)(2,1)} %collective-permute-done.8.other_ref.refs_0_, ...), custom_call_target="tpu_custom_call" | custom-call | flops 1610612736 | bytes 6815744 | tf_op jit(solution)/shard_map/pallas_call | solution.py:445
  393.3 6.7 %collective-permute-done.38 = bf16[384,1024]{1,0:T(8,128)(2,1)S(1)} collective-permute-done((bf16[384,1024]{1,0:T(8,128)(2,1)}, bf16[384,1024]{1,0:T(8,128)(2,1)S(1)}, u32[]{:S(2)}, u32[]{:S(2)}) %collective-permute-start.38) | collective-permute-done | bytes 786464 | tf_op jit(solution)/shard_map/ppermute | solution.py:28
  400.0 2.7 add_convert_fusion.4
  403.0 1.7 collective-permute-start.34
  407.1 5.9 %shard_map.209 = (f32[384,1024]{1,0:T(8,128)}, f32[384,1024]{1,0:T(8,128)}) custom-call(s32[1]{0:T(128)} %bitcast.16.info_ref, bf16[384,1024]{1,0:T(8,128)(2,1)} %shard_map.208.own_ref, bf16[384,1024]{1,0:T(8,128)(2,1)} %copy-done.13, bf16[1024,1024]{1,0:T(8,128)(2,1)} %collective-permute-done.8.other_ref.refs_0_, ...), custom_call_target="tpu_custom_call" | custom-call | flops 1610612736 | bytes 6815744 | tf_op jit(solution)/shard_map/pallas_call | solution.py:445
  413.0 4.0 collective-permute-done.37
  416.9 6.6 %collective-permute-done.39 = bf16[384,1024]{1,0:T(8,128)(2,1)} collective-permute-done((bf16[384,1024]{1,0:T(8,128)(2,1)}, bf16[384,1024]{1,0:T(8,128)(2,1)}, u32[]{:S(2)}, u32[]{:S(2)}) %collective-permute-start.39) | collective-permute-done | bytes 786464 | tf_op jit(solution)/shard_map/ppermute | solution.py:28
  423.5 3.1 add_convert_fusion.3
  426.6 2.5 dynamic-slice_bitcast_fusion.6
  430.9 9.3 %collective-permute-done.34 = bf16[384,1024]{1,0:T(8,128)(2,1)S(1)} collective-permute-done((bf16[384,1024]{1,0:T(8,128)(2,1)}, bf16[384,1024]{1,0:T(8,128)(2,1)S(1)}, u32[]{:S(2)}, u32[]{:S(2)}) %collective-permute-start.34) | collective-permute-done | bytes 786464 | tf_op jit(solution)/shard_map/ppermute | solution.py:28
  442.3 7.2 %collective-permute-done.15 = bf16[96,2048]{1,0:T(8,128)(2,1)} collective-permute-done((bf16[96,2048]{1,0:T(8,128)(2,1)}, bf16[96,2048]{1,0:T(8,128)(2,1)}, u32[]{:S(2)}, u32[]{:S(2)}) %collective-permute-start.15) | collective-permute-done | bytes 393248 | tf_op jit(solution)/shard_map/ppermute | solution.py:28
  450.1 4.7 %collective-permute-done.13 = bf16[96,2048]{1,0:T(8,128)(2,1)} collective-permute-done((bf16[96,2048]{1,0:T(8,128)(2,1)}, bf16[96,2048]{1,0:T(8,128)(2,1)}, u32[]{:S(2)}, u32[]{:S(2)}) %collective-permute-start.13) | collective-permute-done | bytes 393248 | tf_op jit(solution)/shard_map/ppermute | solution.py:28
  454.7 2.2 fusion.1
  457.0 2.0 reshape.309
  (150 shorter events, 46.4 us)
Async XLA Ops:
  5.9 15.1 %all-to-all-start = ((s32[8,1,96]{2,1,0:T(1,128)}), s32[8,1,96]{2,1,0:T(1,128)S(1)}, u32[]{:S(2)}, u32[]{:S(2)}) async-start(s32[8,1,96]{2,1,0:T(1,128)} %all_to_all.13), calls=%async_computation | async-start | bytes 8192 | tf_op jit(solution)/shard_map/all_to_all | solution.py:547
  37.2 79.2 %all-to-all-start.1 = ((bf16[32,24,2048]{2,1,0:T(8,128)(2,1)}), bf16[32,24,2048]{2,1,0:T(8,128)(2,1)S(1)}, u32[]{:S(2)}, u32[]{:S(2)}) async-start(bf16[32,24,2048]{2,1,0:T(8,128)(2,1)} %bitcast.40), calls=%async_computation.1 | async-start | bytes 6291456 | tf_op jit(solution)/shard_map/all_to_all | solution.py:561
  43.3 48.8 %collective-permute-start = (bf16[256,1536]{1,0:T(8,128)(2,1)}, bf16[256,1536]{1,0:T(8,128)(2,1)}, u32[]{:S(2)}, u32[]{:S(2)}) collective-permute-start(bf16[256,1536]{1,0:T(8,128)(2,1)} %get-tuple-element.35), channel_id=1, source_target_pairs={{0,1},{1,0},{2,3},{3,2},{4,5},{5,4},{6,7},{7,6},{8,9},{9,8},{10,11... | collective-permute-start | bytes 2359304 | tf_op jit(solution)/shard_map/ppermute | solution.py:28
  45.1 48.0 %collective-permute-start.1 = (bf16[256,1536]{1,0:T(8,128)(2,1)}, bf16[256,1536]{1,0:T(8,128)(2,1)}, u32[]{:S(2)}, u32[]{:S(2)}) collective-permute-start(bf16[256,1536]{1,0:T(8,128)(2,1)} %get-tuple-element.36), channel_id=1, source_target_pairs={{0,2},{1,3},{2,0},{3,1},{4,6},{5,7},{6,4},{7,5},{8,10},{9,11},{10,... | collective-permute-start | bytes 2359304 | tf_op jit(solution)/shard_map/ppermute | solution.py:28
  46.6 69.8 %collective-permute-start.2 = (bf16[256,1536]{1,0:T(8,128)(2,1)}, bf16[256,1536]{1,0:T(8,128)(2,1)}, u32[]{:S(2)}, u32[]{:S(2)}) collective-permute-start(bf16[256,1536]{1,0:T(8,128)(2,1)} %get-tuple-element.37.other_ref), channel_id=1, source_target_pairs={{0,3},{1,2},{2,1},{3,0},{4,7},{5,6},{6,5},{7,4},{8,11},{9,10},{10,... | collective-permute-start | bytes 2359304 | tf_op jit(solution)/shard_map/ppermute | solution.py:28
  116.4 1.7 copy-start.14
  122.5 48.1 %all-to-all-start.2 = ((bf16[4,96,2048]{2,1,0:T(8,128)(2,1)}), bf16[4,96,2048]{2,1,0:T(8,128)(2,1)S(1)}, u32[]{:S(2)}, u32[]{:S(2)}) async-start(bf16[4,96,2048]{2,1,0:T(8,128)(2,1)} %get-tuple-element.38.other_ref), calls=%async_computation.2 | async-start | bytes 3145728 | tf_op jit(solution)/shard_map/all_to_all | solution.py:569
  130.9 60.3 %collective-permute-start.18 = (bf16[1024,1536]{1,0:T(8,128)(2,1)}, bf16[1024,1536]{1,0:T(8,128)(2,1)}, u32[]{:S(2)}, u32[]{:S(2)}) collective-permute-start(bf16[1024,1536]{1,0:T(8,128)(2,1)} %shard_map.197.refs_4_), channel_id=1, source_target_pairs={{0,4},{4,0},{1,5},{5,1},{2,6},{6,2},{3,7},{7,3},{8,12},{12,8},{9,1... | collective-permute-start | bytes 9437192 | tf_op jit(solution)/shard_map/ppermute | solution.py:556
  137.7 15.8 %collective-permute-start.3 = (bf16[256,1024]{1,0:T(8,128)(2,1)}, bf16[256,1024]{1,0:T(8,128)(2,1)S(1)}, u32[]{:S(2)}, u32[]{:S(2)}) collective-permute-start(bf16[256,1024]{1,0:T(8,128)(2,1)} %shard_map.189), channel_id=1, source_target_pairs={{0,1},{1,0},{2,3},{3,2},{4,5},{5,4},{6,7},{7,6},{8,9},{9,8},{10,11... | collective-permute-start | bytes 1572872 | tf_op jit(solution)/shard_map/ppermute | solution.py:28
  140.5 25.5 %collective-permute-start.4 = (bf16[256,1024]{1,0:T(8,128)(2,1)}, bf16[256,1024]{1,0:T(8,128)(2,1)S(1)}, u32[]{:S(2)}, u32[]{:S(2)}) collective-permute-start(bf16[256,1024]{1,0:T(8,128)(2,1)} %shard_map.190), channel_id=1, source_target_pairs={{0,2},{1,3},{2,0},{3,1},{4,6},{5,7},{6,4},{7,5},{8,10},{9,11},{10,... | collective-permute-start | bytes 1572872 | tf_op jit(solution)/shard_map/ppermute | solution.py:28
  140.5 25.5 %collective-permute-start.5 = (bf16[256,1024]{1,0:T(8,128)(2,1)}, bf16[256,1024]{1,0:T(8,128)(2,1)S(1)}, u32[]{:S(2)}, u32[]{:S(2)}) collective-permute-start(bf16[256,1024]{1,0:T(8,128)(2,1)} %shard_map.191), channel_id=1, source_target_pairs={{0,3},{1,2},{2,1},{3,0},{4,7},{5,6},{6,5},{7,4},{8,11},{9,10},{10,... | collective-permute-start | bytes 1572872 | tf_op jit(solution)/shard_map/ppermute | solution.py:28
  153.5 12.5 %copy-start.16 = (bf16[256,1024]{1,0:T(8,128)(2,1)}, bf16[256,1024]{1,0:T(8,128)(2,1)S(1)}, u32[]{:S(2)}) copy-start(bf16[256,1024]{1,0:T(8,128)(2,1)S(1)} %collective-permute-done.3.refs_1_.other_ref) | copy-start | bytes 1572868
  166.0 1.0 copy-start.18
  170.6 1.2 copy-start.12
  171.7 58.3 %collective-permute-start.6 = (bf16[1024,1024]{1,0:T(8,128)(2,1)}, bf16[1024,1024]{1,0:T(8,128)(2,1)}, u32[]{:S(2)}, u32[]{:S(2)}) collective-permute-start(bf16[1024,1024]{1,0:T(8,128)(2,1)} %shard_map.193.refs_3_), channel_id=1, source_target_pairs={{0,8},{8,16},{16,24},{1,9},{9,17},{17,25},{2,10},{10,18},{18,26},{... | collective-permute-start | bytes 6291464 | tf_op jit(solution)/shard_map/ppermute | solution.py:97
  177.0 55.0 %collective-permute-start.9 = (bf16[1024,1024]{1,0:T(8,128)(2,1)}, bf16[1024,1024]{1,0:T(8,128)(2,1)}, u32[]{:S(2)}, u32[]{:S(2)}) collective-permute-start(bf16[1024,1024]{1,0:T(8,128)(2,1)} %shard_map.193.refs_3_), channel_id=1, source_target_pairs={{8,0},{16,8},{24,16},{9,1},{17,9},{25,17},{10,2},{18,10},{26,18},{... | collective-permute-start | bytes 6291464 | tf_op jit(solution)/shard_map/ppermute | solution.py:98
  189.6 97.7 %copy-start.7 = (bf16[96,2048]{1,0:T(8,128)(2,1)}, bf16[96,2048]{1,0:T(8,128)(2,1)S(1)}, u32[]{:S(2)}) copy-start(bf16[96,2048]{1,0:T(8,128)(2,1)S(1)} %get-tuple-element.69.refs_0_) | copy-start | bytes 1179652
  189.6 19.3 %copy-start = (bf16[1024,1536]{1,0:T(8,128)(2,1)S(1)}, bf16[1024,1536]{1,0:T(8,128)(2,1)}, u32[]{:S(2)}) copy-start(bf16[1024,1536]{1,0:T(8,128)(2,1)} %shard_map.197.refs_4_) | copy-start | bytes 9437188
  189.6 12.3 %collective-permute-start.19 = (bf16[96,2048]{1,0:T(8,128)(2,1)}, bf16[96,2048]{1,0:T(8,128)(2,1)S(1)}, u32[]{:S(2)}, u32[]{:S(2)}) collective-permute-start(bf16[96,2048]{1,0:T(8,128)(2,1)} %shard_map.201.refs_0_), channel_id=1, source_target_pairs={{0,1},{1,0},{2,3},{3,2},{4,5},{5,4},{6,7},{7,6},{8,9},{9,8},{10,11... | collective-permute-start | bytes 1179656 | tf_op jit(solution)/shard_map/ppermute | solution.py:28
  190.0 18.8 %collective-permute-start.20 = (bf16[96,2048]{1,0:T(8,128)(2,1)}, bf16[96,2048]{1,0:T(8,128)(2,1)S(1)}, u32[]{:S(2)}, u32[]{:S(2)}) collective-permute-start(bf16[96,2048]{1,0:T(8,128)(2,1)} %shard_map.201.refs_0_), channel_id=1, source_target_pairs={{0,2},{1,3},{2,0},{3,1},{4,6},{5,7},{6,4},{7,5},{8,10},{9,11},{10,... | collective-permute-start | bytes 1179656 | tf_op jit(solution)/shard_map/ppermute | solution.py:28
  191.2 17.6 %collective-permute-start.21 = (bf16[96,2048]{1,0:T(8,128)(2,1)}, bf16[96,2048]{1,0:T(8,128)(2,1)S(1)}, u32[]{:S(2)}, u32[]{:S(2)}) collective-permute-start(bf16[96,2048]{1,0:T(8,128)(2,1)} %shard_map.201.refs_0_), channel_id=1, source_target_pairs={{0,3},{1,2},{2,1},{3,0},{4,7},{5,6},{6,5},{7,4},{8,11},{9,10},{10,... | collective-permute-start | bytes 1179656 | tf_op jit(solution)/shard_map/ppermute | solution.py:28
  208.8 1.0 copy-start.1
  209.8 10.0 %copy-start.9 = (bf16[96,2048]{1,0:T(8,128)(2,1)S(1)}, bf16[96,2048]{1,0:T(8,128)(2,1)}, u32[]{:S(2)}) copy-start(bf16[96,2048]{1,0:T(8,128)(2,1)} %get-tuple-element.67.refs_0_) | copy-start | bytes 1179652
  214.6 31.2 %copy-start.4 = (bf16[384,1536]{1,0:T(8,128)(2,1)}, bf16[384,1536]{1,0:T(8,128)(2,1)S(1)}, u32[]{:S(2)}) copy-start(bf16[384,1536]{1,0:T(8,128)(2,1)S(1)} %shard_map.202) | copy-start | bytes 3538948
  214.6 32.2 %collective-permute-start.28 = (bf16[384,1536]{1,0:T(8,128)(2,1)S(1)}, bf16[384,1536]{1,0:T(8,128)(2,1)}, u32[]{:S(2)}, u32[]{:S(2)}) collective-permute-start(bf16[384,1536]{1,0:T(8,128)(2,1)S(1)} %shard_map.202), channel_id=1, source_target_pairs={{0,8},{24,16},{1,9},{25,17},{2,10},{26,18},{3,11},{27,19},{4,12},{... | collective-permute-start | bytes 3538952 | tf_op jit(solution)/shard_map/ppermute | solution.py:60
  219.9 8.2 %collective-permute-start.25 = (bf16[96,2048]{1,0:T(8,128)(2,1)S(1)}, bf16[96,2048]{1,0:T(8,128)(2,1)S(1)}, u32[]{:S(2)}, u32[]{:S(2)}) collective-permute-start(bf16[96,2048]{1,0:T(8,128)(2,1)S(1)} %copy-done.9), channel_id=1, source_target_pairs={{0,1},{1,0},{2,3},{3,2},{4,5},{5,4},{6,7},{7,6},{8,9},{9,8},{10,11... | collective-permute-start | bytes 1179656 | tf_op jit(solution)/shard_map/ppermute | solution.py:28
  221.2 13.6 %collective-permute-start.26 = (bf16[96,2048]{1,0:T(8,128)(2,1)S(1)}, bf16[96,2048]{1,0:T(8,128)(2,1)S(1)}, u32[]{:S(2)}, u32[]{:S(2)}) collective-permute-start(bf16[96,2048]{1,0:T(8,128)(2,1)S(1)} %copy-done.9), channel_id=1, source_target_pairs={{0,2},{1,3},{2,0},{3,1},{4,6},{5,7},{6,4},{7,5},{8,10},{9,11},{10,... | collective-permute-start | bytes 1179656 | tf_op jit(solution)/shard_map/ppermute | solution.py:28
  228.1 13.0 %collective-permute-start.27 = (bf16[96,2048]{1,0:T(8,128)(2,1)S(1)}, bf16[96,2048]{1,0:T(8,128)(2,1)S(1)}, u32[]{:S(2)}, u32[]{:S(2)}) collective-permute-start(bf16[96,2048]{1,0:T(8,128)(2,1)S(1)} %copy-done.9), channel_id=1, source_target_pairs={{0,3},{1,2},{2,1},{3,0},{4,7},{5,6},{6,5},{7,4},{8,11},{9,10},{10,... | collective-permute-start | bytes 1179656 | tf_op jit(solution)/shard_map/ppermute | solution.py:28
  230.0 46.9 %collective-permute-start.7 = (bf16[1024,1024]{1,0:T(8,128)(2,1)}, bf16[1024,1024]{1,0:T(8,128)(2,1)}, u32[]{:S(2)}, u32[]{:S(2)}) collective-permute-start(bf16[1024,1024]{1,0:T(8,128)(2,1)} %collective-permute-done.6.other_ref.refs_2_), channel_id=1, source_target_pairs={{8,16},{16,24},{9,17},{17,25},{10,18},{18,26},{11,19},{19,27},{12,... | collective-permute-start | bytes 6291464 | tf_op jit(solution)/shard_map/ppermute | solution.py:97
  232.0 46.9 %collective-permute-start.10 = (bf16[1024,1024]{1,0:T(8,128)(2,1)}, bf16[1024,1024]{1,0:T(8,128)(2,1)}, u32[]{:S(2)}, u32[]{:S(2)}) collective-permute-start(bf16[1024,1024]{1,0:T(8,128)(2,1)} %collective-permute-done.9.refs_4_), channel_id=1, source_target_pairs={{8,0},{16,8},{9,1},{17,9},{10,2},{18,10},{11,3},{19,11},{12,4},{20... | collective-permute-start | bytes 6291464 | tf_op jit(solution)/shard_map/ppermute | solution.py:98
  234.8 20.9 %collective-permute-start.22 = (bf16[96,2048]{1,0:T(8,128)(2,1)}, bf16[96,2048]{1,0:T(8,128)(2,1)}, u32[]{:S(2)}, u32[]{:S(2)}) collective-permute-start(bf16[96,2048]{1,0:T(8,128)(2,1)} %get-tuple-element.66.refs_0_), channel_id=1, source_target_pairs={{0,1},{1,0},{2,3},{3,2},{4,5},{5,4},{6,7},{7,6},{8,9},{9,8},{10,11... | collective-permute-start | bytes 1179656 | tf_op jit(solution)/shard_map/ppermute | solution.py:28
  245.7 1.0 copy-start.3
  249.7 37.6 %collective-permute-start.29 = (bf16[384,1536]{1,0:T(8,128)(2,1)}, bf16[384,1536]{1,0:T(8,128)(2,1)}, u32[]{:S(2)}, u32[]{:S(2)}) collective-permute-start(bf16[384,1536]{1,0:T(8,128)(2,1)} %add_convert_fusion.2), channel_id=1, source_target_pairs={{0,8},{8,16},{1,9},{9,17},{2,10},{10,18},{3,11},{11,19},{4,12},{12... | collective-permute-start | bytes 3538952 | tf_op jit(solution)/shard_map/ppermute | solution.py:63
  254.1 34.6 %collective-permute-start.31 = (bf16[384,1536]{1,0:T(8,128)(2,1)}, bf16[384,1536]{1,0:T(8,128)(2,1)}, u32[]{:S(2)}, u32[]{:S(2)}) collective-permute-start(bf16[384,1536]{1,0:T(8,128)(2,1)} %add_convert_fusion.2), channel_id=1, source_target_pairs={{24,16},{16,8},{25,17},{17,9},{26,18},{18,10},{27,19},{19,11},{28,... | collective-permute-start | bytes 3538952 | tf_op jit(solution)/shard_map/ppermute | solution.py:64
  255.8 9.4 %collective-permute-start.23 = (bf16[96,2048]{1,0:T(8,128)(2,1)}, bf16[96,2048]{1,0:T(8,128)(2,1)S(1)}, u32[]{:S(2)}, u32[]{:S(2)}) collective-permute-start(bf16[96,2048]{1,0:T(8,128)(2,1)} %get-tuple-element.66.refs_0_), channel_id=1, source_target_pairs={{0,2},{1,3},{2,0},{3,1},{4,6},{5,7},{6,4},{7,5},{8,10},{9,11},{10,... | collective-permute-start | bytes 1179656 | tf_op jit(solution)/shard_map/ppermute | solution.py:28
  266.0 9.8 %collective-permute-start.24 = (bf16[96,2048]{1,0:T(8,128)(2,1)}, bf16[96,2048]{1,0:T(8,128)(2,1)}, u32[]{:S(2)}, u32[]{:S(2)}) collective-permute-start(bf16[96,2048]{1,0:T(8,128)(2,1)} %get-tuple-element.66.refs_0_), channel_id=1, source_target_pairs={{0,3},{1,2},{2,1},{3,0},{4,7},{5,6},{6,5},{7,4},{8,11},{9,10},{10,... | collective-permute-start | bytes 1179656 | tf_op jit(solution)/shard_map/ppermute | solution.py:28
  275.7 35.6 %collective-permute-start.16 = (bf16[96,2048]{1,0:T(8,128)(2,1)S(1)}, bf16[96,2048]{1,0:T(8,128)(2,1)}, u32[]{:S(2)}, u32[]{:S(2)}) collective-permute-start(bf16[96,2048]{1,0:T(8,128)(2,1)S(1)} %get-tuple-element.69.refs_0_), channel_id=1, source_target_pairs={{0,1},{1,0},{2,3},{3,2},{4,5},{5,4},{6,7},{7,6},{8,9},{9,8},{10,11... | collective-permute-start | bytes 1179656 | tf_op jit(solution)/shard_map/ppermute | solution.py:28
  277.0 53.9 %collective-permute-start.8 = (bf16[1024,1024]{1,0:T(8,128)(2,1)}, bf16[1024,1024]{1,0:T(8,128)(2,1)}, u32[]{:S(2)}, u32[]{:S(2)}) collective-permute-start(bf16[1024,1024]{1,0:T(8,128)(2,1)} %collective-permute-done.7.other_ref.refs_1_), channel_id=1, source_target_pairs={{16,24},{17,25},{18,26},{19,27},{20,28},{21,29},{22,30},{23,31}} | collective-permute-start | bytes 6291464 | tf_op jit(solution)/shard_map/ppermute | solution.py:97
  278.9 52.1 %collective-permute-start.11 = (bf16[1024,1024]{1,0:T(8,128)(2,1)}, bf16[1024,1024]{1,0:T(8,128)(2,1)}, u32[]{:S(2)}, u32[]{:S(2)}) collective-permute-start(bf16[1024,1024]{1,0:T(8,128)(2,1)} %collective-permute-done.10.refs_5_), channel_id=1, source_target_pairs={{8,0},{9,1},{10,2},{11,3},{12,4},{13,5},{14,6},{15,7}} | collective-permute-start | bytes 6291464 | tf_op jit(solution)/shard_map/ppermute | solution.py:98
  280.2 1.0 copy-start.11
  286.3 1.0 copy-start.5
  287.3 27.2 %collective-permute-start.17 = (bf16[96,2048]{1,0:T(8,128)(2,1)S(1)}, bf16[96,2048]{1,0:T(8,128)(2,1)}, u32[]{:S(2)}, u32[]{:S(2)}) collective-permute-start(bf16[96,2048]{1,0:T(8,128)(2,1)S(1)} %get-tuple-element.69.refs_0_), channel_id=1, source_target_pairs={{0,2},{1,3},{2,0},{3,1},{4,6},{5,7},{6,4},{7,5},{8,10},{9,11},{10,... | collective-permute-start | bytes 1179656 | tf_op jit(solution)/shard_map/ppermute | solution.py:28
  288.6 24.0 %copy-start.22 = (s32[96]{0:T(128)S(1)}, s32[96]{0:T(128)}, u32[]{:S(2)}) copy-start(s32[96]{0:T(128)} %lengths_ref.1) | copy-start | bytes 1156
  293.1 38.8 %collective-permute-start.30 = (bf16[384,1536]{1,0:T(8,128)(2,1)}, bf16[384,1536]{1,0:T(8,128)(2,1)}, u32[]{:S(2)}, u32[]{:S(2)}) collective-permute-start(bf16[384,1536]{1,0:T(8,128)(2,1)} %get-tuple-element.61), channel_id=1, source_target_pairs={{0,8},{8,16},{16,24},{1,9},{9,17},{17,25},{2,10},{10,18},{18,26},{... | collective-permute-start | bytes 3538952 | tf_op jit(solution)/shard_map/ppermute | solution.py:68
  311.4 39.1 %collective-permute-start.32 = (bf16[384,1536]{1,0:T(8,128)(2,1)}, bf16[384,1536]{1,0:T(8,128)(2,1)}, u32[]{:S(2)}, u32[]{:S(2)}) collective-permute-start(bf16[384,1536]{1,0:T(8,128)(2,1)} %get-tuple-element.60), channel_id=1, source_target_pairs={{24,16},{16,8},{8,0},{25,17},{17,9},{9,1},{26,18},{18,10},{10,2},{... | collective-permute-start | bytes 3538952 | tf_op jit(solution)/shard_map/ppermute | solution.py:71
  314.5 9.0 %collective-permute-start.12 = (bf16[96,2048]{1,0:T(8,128)(2,1)}, bf16[96,2048]{1,0:T(8,128)(2,1)S(1)}, u32[]{:S(2)}, u32[]{:S(2)}) collective-permute-start(bf16[96,2048]{1,0:T(8,128)(2,1)} %copy-done.7), channel_id=1, source_target_pairs={{0,3},{1,2},{2,1},{3,0},{4,7},{5,6},{6,5},{7,4},{8,11},{9,10},{10,... | collective-permute-start | bytes 1179656 | tf_op jit(solution)/shard_map/ppermute | solution.py:28
  323.5 1.0 copy-start.8
  324.4 5.1 %copy-start.6 = (bf16[96,2048]{1,0:T(8,128)(2,1)}, bf16[96,2048]{1,0:T(8,128)(2,1)S(1)}, u32[]{:S(2)}) copy-start(bf16[96,2048]{1,0:T(8,128)(2,1)S(1)} %collective-permute-done.12.other_ref.refs_3_) | copy-start | bytes 1179652
  329.5 1.4 copy-start.2
  370.3 2.5 collective-permute-start.33
  372.8 0.9 copy-start.13
  379.3 20.7 %collective-permute-start.38 = (bf16[384,1024]{1,0:T(8,128)(2,1)}, bf16[384,1024]{1,0:T(8,128)(2,1)S(1)}, u32[]{:S(2)}, u32[]{:S(2)}) collective-permute-start(bf16[384,1024]{1,0:T(8,128)(2,1)} %get-tuple-element.52), channel_id=1, source_target_pairs={{0,2},{1,3},{2,0},{3,1},{4,6},{5,7},{6,4},{7,5},{8,10},{9,11},{10,... | collective-permute-start | bytes 2359304 | tf_op jit(solution)/shard_map/ppermute | solution.py:28
  380.6 24.2 %collective-permute-start.35 = (bf16[384,1024]{1,0:T(8,128)(2,1)}, bf16[384,1024]{1,0:T(8,128)(2,1)S(1)}, u32[]{:S(2)}, u32[]{:S(2)}) collective-permute-start(bf16[384,1024]{1,0:T(8,128)(2,1)} %get-tuple-element.48), channel_id=1, source_target_pairs={{0,1},{1,0},{2,3},{3,2},{4,5},{5,4},{6,7},{7,6},{8,9},{9,8},{10,11... | collective-permute-start | bytes 2359304 | tf_op jit(solution)/shard_map/ppermute | solution.py:28
  386.5 30.4 %collective-permute-start.37 = (bf16[384,1024]{1,0:T(8,128)(2,1)}, bf16[384,1024]{1,0:T(8,128)(2,1)}, u32[]{:S(2)}, u32[]{:S(2)}) collective-permute-start(bf16[384,1024]{1,0:T(8,128)(2,1)} %get-tuple-element.50), channel_id=1, source_target_pairs={{0,2},{1,3},{2,0},{3,1},{4,6},{5,7},{6,4},{7,5},{8,10},{9,11},{10,... | collective-permute-start | bytes 2359304 | tf_op jit(solution)/shard_map/ppermute | solution.py:28
  400.0 4.8 %copy-start.19 = (f32[384,1024]{1,0:T(8,128)S(1)}, f32[384,1024]{1,0:T(8,128)}, u32[]{:S(2)}) copy-start(f32[384,1024]{1,0:T(8,128)} %get-tuple-element.47) | copy-start | bytes 4718596
  402.7 20.8 %collective-permute-start.39 = (bf16[384,1024]{1,0:T(8,128)(2,1)}, bf16[384,1024]{1,0:T(8,128)(2,1)}, u32[]{:S(2)}, u32[]{:S(2)}) collective-permute-start(bf16[384,1024]{1,0:T(8,128)(2,1)} %add_convert_fusion.4), channel_id=1, source_target_pairs={{0,1},{1,0},{2,3},{3,2},{4,5},{5,4},{6,7},{7,6},{8,9},{9,8},{10,11... | collective-permute-start | bytes 2359304 | tf_op jit(solution)/shard_map/ppermute | solution.py:28
  403.0 37.3 %collective-permute-start.34 = (bf16[384,1024]{1,0:T(8,128)(2,1)}, bf16[384,1024]{1,0:T(8,128)(2,1)S(1)}, u32[]{:S(2)}, u32[]{:S(2)}) collective-permute-start(bf16[384,1024]{1,0:T(8,128)(2,1)} %get-tuple-element.46), channel_id=1, source_target_pairs={{0,1},{1,0},{2,3},{3,2},{4,5},{5,4},{6,7},{7,6},{8,9},{9,8},{10,11... | collective-permute-start | bytes 2359304 | tf_op jit(solution)/shard_map/ppermute | solution.py:28
  405.9 34.7 %collective-permute-start.36 = (bf16[384,1024]{1,0:T(8,128)(2,1)}, bf16[384,1024]{1,0:T(8,128)(2,1)S(1)}, u32[]{:S(2)}, u32[]{:S(2)}) collective-permute-start(bf16[384,1024]{1,0:T(8,128)(2,1)} %add_convert_fusion.5), channel_id=1, source_target_pairs={{0,2},{1,3},{2,0},{3,1},{4,6},{5,7},{6,4},{7,5},{8,10},{9,11},{10,... | collective-permute-start | bytes 2359304 | tf_op jit(solution)/shard_map/ppermute | solution.py:28
  426.6 14.3 %collective-permute-start.40 = (bf16[384,1024]{1,0:T(8,128)(2,1)}, bf16[384,1024]{1,0:T(8,128)(2,1)}, u32[]{:S(2)}, u32[]{:S(2)}) collective-permute-start(bf16[384,1024]{1,0:T(8,128)(2,1)} %add_convert_fusion.3), channel_id=1, source_target_pairs={{0,4},{4,0},{1,5},{5,1},{2,6},{6,2},{3,7},{7,3},{8,12},{12,8},{9,1... | collective-permute-start | bytes 2359304 | tf_op jit(solution)/shard_map/ppermute | solution.py:493
  426.6 13.9 %copy-start.20 = (f32[384,1024]{1,0:T(8,128)S(1)}, f32[384,1024]{1,0:T(8,128)}, u32[]{:S(2)}) copy-start(f32[384,1024]{1,0:T(8,128)} %get-tuple-element.45) | copy-start | bytes 4718596
  429.1 20.3 %collective-permute-start.15 = (bf16[96,2048]{1,0:T(8,128)(2,1)}, bf16[96,2048]{1,0:T(8,128)(2,1)}, u32[]{:S(2)}, u32[]{:S(2)}) collective-permute-start(bf16[96,2048]{1,0:T(8,128)(2,1)} %get-tuple-element.63), channel_id=1, source_target_pairs={{0,3},{1,2},{2,1},{3,0},{4,7},{5,6},{6,5},{7,4},{8,11},{9,10},{10,... | collective-permute-start | bytes 1179656 | tf_op jit(solution)/shard_map/ppermute | solution.py:28
  430.1 20.0 %collective-permute-start.14 = (bf16[96,2048]{1,0:T(8,128)(2,1)}, bf16[96,2048]{1,0:T(8,128)(2,1)}, u32[]{:S(2)}, u32[]{:S(2)}) collective-permute-start(bf16[96,2048]{1,0:T(8,128)(2,1)} %get-tuple-element.64), channel_id=1, source_target_pairs={{0,2},{1,3},{2,0},{3,1},{4,6},{5,7},{6,4},{7,5},{8,10},{9,11},{10,... | collective-permute-start | bytes 1179656 | tf_op jit(solution)/shard_map/ppermute | solution.py:28
  440.2 14.5 %collective-permute-start.13 = (bf16[96,2048]{1,0:T(8,128)(2,1)}, bf16[96,2048]{1,0:T(8,128)(2,1)}, u32[]{:S(2)}, u32[]{:S(2)}) collective-permute-start(bf16[96,2048]{1,0:T(8,128)(2,1)} %get-tuple-element.65), channel_id=1, source_target_pairs={{0,1},{1,0},{2,3},{3,2},{4,5},{5,4},{6,7},{7,6},{8,9},{9,8},{10,11... | collective-permute-start | bytes 1179656 | tf_op jit(solution)/shard_map/ppermute | solution.py:28
  440.9 13.9 %copy-start.15 = (bf16[384,384]{1,0:T(8,128)(2,1)S(1)}, bf16[384,384]{1,0:T(8,128)(2,1)}, u32[]{:S(2)}) copy-start(bf16[384,384]{1,0:T(8,128)(2,1)} %shard_map.195.back_ref) | copy-start | bytes 884740
  (3 other events, 2.2 us)

commit v2 on v1

--- a/solution.py
+++ b/solution.py
@@ -54,15 +54,13 @@
     return np.array(order, dtype=np.int32)
 
 
-def line_sum(products, place, count, gates):
+def line_sum(products, place, count):
     if count == 4:
         first, second, third, own = products
         one = lax.ppermute(first, "z", [(0, 1), (3, 2)])
-        one = after(one, gates[0])
         block = (second.astype(f32) + one.astype(f32)).astype(bf16)
         up = lax.ppermute(block, "z", [(0, 1), (1, 2)])
         down = lax.ppermute(block, "z", [(3, 2), (2, 1)])
-        up = after(up, gates[1])
         rest = jnp.where(place == 2, first, third).astype(f32)
         block = (rest + up.astype(f32)).astype(bf16)
         up = lax.ppermute(block, "z", [(0, 1), (1, 2), (2, 3)])
@@ -90,14 +88,10 @@
     return products[-1], arrived[0], arrived[1]
 
 
-def line_gather(block, count):
-    blocks = {0: block}
-    up = down = block
-    for step in range(1, count):
-        up = lax.ppermute(up, "z", [(i, i + 1) for i in range(step - 1, count - 1)])
-        down = lax.ppermute(down, "z", [(i, i - 1) for i in range(1, count - step + 1)])
-        blocks[-step], blocks[step] = up, down
-    return blocks
+def pass_on(up, down, step, count):
+    up = lax.ppermute(up, "z", [(i, i + 1) for i in range(step - 1, count - 1)])
+    down = lax.ppermute(down, "z", [(i, i - 1) for i in range(1, count - step + 1)])
+    return up, down
 
 
 def blend_kernel(widths, place_ref, *refs):
@@ -308,7 +302,7 @@
             jax.ShapeDtypeStruct((query_blocks, tokens, HEAD_WIDTH), bf16),
             jax.ShapeDtypeStruct((tokens, (blocks - query_blocks) * HEAD_WIDTH), bf16),
         ],
-        compiler_params=pltpu.CompilerParams(vmem_limit_bytes=VMEM),
+        compiler_params=pltpu.CompilerParams(vmem_limit_bytes=16 * 1024 * 1024),
         cost_estimate=pl.CostEstimate(
             flops=2 * tokens * tokens * width,
             bytes_accessed=10 * tokens * width,
@@ -396,7 +390,7 @@
     heads, tokens = queries.shape[0], queries.shape[1]
     row_count, slots, width = key_cache.shape
     groups = width // HEAD_WIDTH
-    rows = 8
+    rows = 16 if row_count % 16 == 0 else 8
     held = rows * DECODE_STEPS
     return pl.pallas_call(
         functools.partial(attend_kernel, rows, groups),
@@ -423,36 +417,41 @@
 def term_kernel(places, info_ref, own_ref, other_ref, *refs):
     blocks = refs[: len(places)]
     own_out_ref, other_out_ref, weights_ref, arrival = refs[len(places) :]
+    step = pl.program_id(0)
     for place, block in zip(places, blocks):
 
-        @pl.when(info_ref[0] == place)
+        @pl.when((info_ref[0] == place) & (step == 0))
         def _(block=block):
             copy = pltpu.make_async_copy(block, weights_ref, arrival)
             copy.start()
             copy.wait()
 
-    weights = weights_ref[...]
-    for rows_ref, out_ref in ((own_ref, own_out_ref), (other_ref, other_out_ref)):
-        product = jnp.dot(rows_ref[...], weights, preferred_element_type=f32)
-        out_ref[...] = product.astype(out_ref.dtype)
+    for at, rows_ref, out_ref in ((0, own_ref, own_out_ref), (1, other_ref, other_out_ref)):
+
+        @pl.when(step == at)
+        def _(rows_ref=rows_ref, out_ref=out_ref):
+            product = jnp.dot(rows_ref[...], weights_ref[...], preferred_element_type=f32)
+            out_ref[...] = product.astype(out_ref.dtype)
 
 
 def term(own, other, blocks, place, own_type, other_type):
     places = sorted(blocks)
     depth, height = blocks[0].shape
     tokens = own.shape[0]
-    whole = pl.BlockSpec(memory_space=pltpu.VMEM)
+    rows = pl.BlockSpec((tokens, depth), lambda i: (0, 0))
+    sums = pl.BlockSpec((tokens, height), lambda i: (0, 0))
     return pl.pallas_call(
         functools.partial(term_kernel, places),
-        in_specs=[pl.BlockSpec(memory_space=pltpu.SMEM), whole, whole]
+        grid=(2,),
+        in_specs=[pl.BlockSpec(memory_space=pltpu.SMEM), rows, rows]
         + [pl.BlockSpec(memory_space=pl.ANY)] * len(places),
-        out_specs=[whole, whole],
+        out_specs=[sums, sums],
         out_shape=[
             jax.ShapeDtypeStruct((tokens, height), own_type),
             jax.ShapeDtypeStruct((tokens, height), other_type),
         ],
         scratch_shapes=[pltpu.VMEM((depth, height), bf16), pltpu.SemaphoreType.DMA],
-        compiler_params=pltpu.CompilerParams(vmem_limit_bytes=VMEM),
+        compiler_params=pltpu.CompilerParams(vmem_limit_bytes=24 * 1024 * 1024),
         cost_estimate=pl.CostEstimate(
             flops=4 * tokens * height * depth,
             bytes_accessed=2 * height * depth + 12 * tokens * height,
@@ -464,9 +463,9 @@
 def sum_over_tensor(attended, blocks, t_at, z_at, core_at, count):
     other = lax.ppermute(attended, "core", [(0, 1), (1, 0)])
 
-    def of(bits, own_type, other_type):
+    def of(bits, own_type, other_type, own=attended, other=other):
         place = jnp.bitwise_xor(t_at, bits) - z_at
-        return term(attended, other, blocks, place, own_type, other_type)
+        return term(own, other, blocks, place, own_type, other_type)
 
     if count == 4:
         far_own, far_other = of(3, bf16, bf16)
@@ -477,7 +476,7 @@
         near_other = swap(near_other, 2, count)
         pass_other = swap((pass_other + far_other.astype(f32)).astype(bf16), 1, count)
         pass_own = swap((pass_own + far_own.astype(f32)).astype(bf16), 2, count)
-        sum_own, sum_other = of(0, f32, f32)
+        sum_own, sum_other = of(0, f32, f32, after(attended, near_own), after(other, near_other))
         sum_other = sum_other + near_other.astype(f32) + pass_other.astype(f32)
         sum_own = sum_own + near_own.astype(f32) + pass_own.astype(f32)
     else:
@@ -546,16 +545,13 @@
     ).reshape(n_r, capacity)
     asked = lax.all_to_all(wanted, ("z", "core"), 0, 0, tiled=True)
 
+    (next_o,), o_columns = blend((teacher_o,), (student_o,), t_at, n_t)
     (next_q, next_k, next_v), qkv_columns = blend(
         (teacher_q, teacher_k, teacher_v), (student_q, student_k, student_v), t_at, n_t
     )
-    (next_o,), o_columns = blend((teacher_o,), (student_o,), t_at, n_t)
-    qkv_by_bits = [x if b == 0 else swap(x, b, n_t) for b, x in enumerate(qkv_columns)]
-
-    weights = in_order(qkv_by_bits, t_at)
-    other = lax.ppermute(weights, "core", [(0, 1), (1, 0)])
-
-    asked = after(asked, qkv_columns[-1])
+    o_by_bits = [x if b == 0 else swap(x, b, n_t) for b, x in enumerate(o_columns)]
+
+    asked = after(asked, o_columns[-1])
     picked = jnp.take(embedding, asked.reshape(-1), axis=0, mode="clip")
     picked = picked.reshape(n_r * n_t, quarter_slots, feature_block)
     landed = lax.all_to_all(picked, ("z", "core", "tensor"), 0, 0, tiled=True)
@@ -563,37 +559,6 @@
     source = jnp.sum(jnp.where(mine, (owner * quarter_slots + slot)[None, :], 0), axis=1)
     choose = (source[:, None] == jnp.arange(n_r * quarter_slots)[None, :]).astype(bf16)
     landed = landed.reshape(n_r, n_t, quarter_slots, feature_block)
-    for columns in qkv_by_bits[1:]:
-        choose = after(choose, columns)
-    raw, normed = normalize(choose, landed, norm_gain, core_at, n_z)
-    held = lax.all_to_all(normed, "z", 0, 0, tiled=True)
-
-    o_by_bits = [
-        x if b == 0 else swap(after(x, normed), b, n_t) for b, x in enumerate(o_columns)
-    ]
-    rows_o = in_order(o_by_bits, t_at, turned=True)
-
-    order = jnp.asarray(due_order(n_z))[z_at]
-    products = []
-    for k in range(n_z):
-        chunk = lax.dynamic_index_in_dim(held, order[k], 0, keepdims=False)
-        if k == 0:
-            for columns in o_by_bits[1:]:
-                chunk = after(chunk, columns)
-        chunk = [chunk] + [swap(chunk, b, n_t) for b in range(1, n_t)]
-        last = chunk[-1]
-        products.append(multiply(chunk, weights, other, f32 if k == n_z - 1 else bf16))
-    blocks_o = line_gather(after(rows_o, held), n_z)
-    gates = [blocks_o[-step] for step in range(1, n_z)]
-    own, up, down = line_sum(products, z_at, n_z, gates)
-
-    raw = after(raw, last)
-    raw_by_bits = []
-    for b in range(n_t):
-        block = lax.dynamic_index_in_dim(raw, jnp.bitwise_xor(t_at, b), 0, keepdims=False)
-        raw_by_bits.append(block if b == 0 else swap(block, b, n_t))
-    residual = jnp.concatenate(raw_by_bits, axis=0)
-
     column = jnp.bitwise_xor(part, t_at) * quarter + spot
     back = column[:, None] == jnp.arange(tokens)[None, :]
     positions = (cache_lengths[:, None] + jnp.arange(steps, dtype=jnp.int32)[None, :]).reshape(-1)
@@ -603,13 +568,55 @@
     cosine_table, sine_table = jnp.cos(angles), jnp.sin(angles)
     cosine_table = jnp.concatenate([cosine_table, cosine_table], axis=1)
     sine_table = jnp.concatenate([-sine_table, sine_table], axis=1)
+
+    rows_o = in_order(o_by_bits, t_at, turned=True)
+    for earlier in (rows_o, cosine_table, sine_table, qkv_columns[0]):
+        choose = after(choose, earlier)
+    raw, normed = normalize(choose, landed, norm_gain, core_at, n_z)
+    held = lax.all_to_all(normed, "z", 0, 0, tiled=True)
+
+    qkv_by_bits = [
+        x if b == 0 else swap(after(x, normed), b, n_t) for b, x in enumerate(qkv_columns)
+    ]
+    order = [
+        sum(jnp.where(z_at == z, int(place), 0) for z, place in enumerate(column))
+        for column in due_order(n_z).T
+    ]
+    chunks = [lax.dynamic_index_in_dim(held, place, 0, keepdims=False) for place in order]
+    weights = in_order([after(qkv_by_bits[0], chunks[0])] + qkv_by_bits[1:], t_at)
+    other = lax.ppermute(weights, "core", [(0, 1), (1, 0)])
+    rows_o = after(rows_o, chunks[0])
+    blocks_o = {0: rows_o}
+    up_o, down_o = pass_on(rows_o, rows_o, 1, n_z)
+    products = []
+    for k in range(n_z):
+        chunk = [chunks[k]] + [swap(chunks[k], b, n_t) for b in range(1, n_t)]
+        last = chunk[-1]
+        if k == n_z - 1:
+            weights = after(after(weights, blocks_o[-2]), blocks_o[2])
+        products.append(multiply(chunk, weights, other, f32 if k == n_z - 1 else bf16))
+        if k == 0:
+            up_o, down_o = after(up_o, products[0]), after(down_o, products[0])
+            blocks_o[-1], blocks_o[1] = up_o, down_o
+            for step in range(2, n_z):
+                up_o, down_o = pass_on(up_o, down_o, step, n_z)
+                blocks_o[-step], blocks_o[step] = up_o, down_o
+    own, up, down = line_sum(products, z_at, n_z)
+
+    raw = after(raw, last)
+    raw_by_bits = []
+    for b in range(n_t):
+        block = lax.dynamic_index_in_dim(raw, jnp.bitwise_xor(t_at, b), 0, keepdims=False)
+        raw_by_bits.append(block if b == 0 else swap(block, b, n_t))
+    residual = jnp.concatenate(raw_by_bits, axis=0)
+
     back = after(after(back.astype(bf16), blocks_o[1 - n_z]), blocks_o[n_z - 1])
     residual = jnp.dot(back, residual, preferred_element_type=f32)
 
     q_width = teacher_q.shape[1] // n_t
     k_width = teacher_k.shape[1] // n_t
     queries, fresh = finish_projection(
-        own,
+        after(own, residual),
         up,
         down,
         cosine_table,

time: 461 us -> 431 us (0.935)
  Pallas kernels: 89.6 us -> 74.8 us
  waiting for transfers between devices: 206 us -> 194 us
  local copies, waits for them, and re-layouts: 39.6 us -> 47.9 us
  between operations: 8.48 us -> 1.26 us
    ppermute x27, waiting for transfers between devices: 184 us -> 122 us  [swap(): return lax.ppermute(values, 'tensor', [(i, i ^ bits) for i in range(count)])]
    all_to_all x1, waiting for transfers between devices: 0.01 us -> 33.4 us  [body(): held = lax.all_to_all(normed, 'z', 0, 0, tiled=True)]
    ppermute x6, waiting for transfers between devices: 0.1 us -> 24.8 us  [the longest x3 24.8 us: pass_on(): lax.ppermute(down, 'z', [(i, i - 1) for i in range(1, count - step + 1)])]
    ppermute x1, waiting for transfers between devices: 18.5 us -> 3.16 us  [line_sum(): down = lax.ppermute(block, 'z', [(3, 2), (2, 1), (1, 0)])]
    unnamed x47 -> x79, local copies, waits for them, and re-layouts: 13.3 us -> 24.9 us
    all_to_all x1, waiting for transfers between devices: 0.01 us -> 8.18 us  [body(): landed = lax.all_to_all(picked, ('z', 'core', 'tensor'), 0, 0, tiled=True)]
    ppermute x1, starting transfers between devices: 18.3 us -> 10.2 us  [line_sum(): up = lax.ppermute(block, 'z', [(0, 1), (1, 2), (2, 3)])]
    pallas_call x4, Pallas kernels: 23.1 us -> 15.8 us  [term(): pl.pallas_call(functools.partial(term_kernel, places), grid=(2,), in_spec...]
  transfers between devices with their start and end apart: 44 -> 44, of which waited for: 24 -> 20; matrix products, arithmetic and copies ran while one was open for 6% -> 6% of each run, Pallas kernels for 13% -> 11%
where the time goes in v2:
time: 431 us; the launch traced here: 428 us
  waiting for transfers between devices  194 us (45%)
  starting transfers between devices  86.5 us (20%)
  Pallas kernels  74.8 us (17%)
  local copies, waits for them, and re-layouts  47.9 us (11%)
  other arithmetic  20 us (5%)
    ppermute x27, waiting for transfers between devices, swap(): return lax.ppermute(values, 'tensor', [(i, i ^ bits) for i in range(count)])  122 us
    ppermute x27, starting transfers between devices, swap(): return lax.ppermute(values, 'tensor', [(i, i ^ bits) for i in range(count)])  34.6 us
    all_to_all x1, waiting for transfers between devices, body(): held = lax.all_to_all(normed, 'z', 0, 0, tiled=True)  33.4 us
    unnamed x79, local copies, waits for them, and re-layouts  24.9 us
    ppermute x3, waiting for transfers between devices, pass_on(): lax.ppermute(down, 'z', [(i, i - 1) for i in range(1, count - step + 1)])  24.8 us
    pallas_call x4, Pallas kernels, multiply(): pl.pallas_call(functools.partial(multiply_kernel, count), grid=(width //...  18.9 us
    pallas_call x4, Pallas kernels, term(): pl.pallas_call(functools.partial(term_kernel, places), grid=(2,), in_spec...  15.8 us
    pallas_call x2, Pallas kernels, blend(): pl.pallas_call(functools.partial(blend_kernel, widths), grid_spec=pltpu.P...  15.6 us
  transfers between devices with their start and end apart: 44, of which 20 were waited for; matrix products, arithmetic and copies ran while one was open for 6% of the time, Pallas kernels for 11%

profile of v2, /device:TPU:0, one launch (start us, length us, event | category | flops | bytes accessed | tf_op | source)
XLA Modules:
  0.0 428.1 jit_solution(3547252339468340546)
XLA Ops:
  5.8 6.3 %all-to-all-start = ((s32[8,1,96]{2,1,0:T(1,128)}), s32[8,1,96]{2,1,0:T(1,128)S(1)}, u32[]{:S(2)}, u32[]{:S(2)}) async-start(s32[8,1,96]{2,1,0:T(1,128)} %all_to_all.13), calls=%async_computation | async-start | bytes 8192 | tf_op jit(solution)/shard_map/all_to_all | solution.py:546
  12.2 6.8 %shard_map.174 = (f32[256,4096]{1,0:T(8,128)}, bf16[256,1024]{1,0:T(8,128)(2,1)}, bf16[256,1024]{1,0:T(8,128)(2,1)}, bf16[256,1024]{1,0:T(8,128)(2,1)}, bf16[256,1024]{1,0:T(8,128)(2,1)}) custom-call(s32[1]{0:T(128)} %bitcast.place_ref, f32[256,4096]{1,0:T(8,128)} %refs_0_.3, f32[256,4096]{1,0:T(8,128)} %refs_1_.3), custom_call_target="tpu_custom_call" | custom-call | flops 3145728 | bytes 14680064 | tf_op jit(solution)/shard_map/pallas_call | solution.py:123
  20.3 14.9 %gather_fusion = bf16[768,2048]{1,0:T(8,128)(2,1)} fusion(bf16[4008,2048]{1,0:T(8,128)(2,1)} %param.16, s32[1024]{0:T(1024)S(1)} %pad_clamp_fusion), kind=kCustom, calls=%fused_computation | custom fusion | bytes 6294528 | tf_op jit(solution)/shard_map/jit(_take)/gather | solution.py:555
  35.2 6.1 %all-to-all-start.1 = ((bf16[32,24,2048]{2,1,0:T(8,128)(2,1)}), bf16[32,24,2048]{2,1,0:T(8,128)(2,1)S(1)}, u32[]{:S(2)}, u32[]{:S(2)}) async-start(bf16[32,24,2048]{2,1,0:T(8,128)(2,1)} %bitcast.36), calls=%async_computation.1 | async-start | bytes 6291456 | tf_op jit(solution)/shard_map/all_to_all | solution.py:557
  41.3 2.7 collective-permute-start.2
  45.2 8.9 %shard_map.173 = (f32[256,4096]{1,0:T(8,128)}, f32[256,1024]{1,0:T(8,128)}, f32[256,1024]{1,0:T(8,128)}, bf16[256,1536]{1,0:T(8,128)(2,1)}, bf16[256,1536]{1,0:T...) custom-call(s32[1]{0:T(128)} %bitcast.place_ref, f32[256,4096]{1,0:T(8,128)} %refs_0_.2, ...), custom_call_target="tpu_custom_call" | custom-call | flops 4718592 | bytes 22020096 | tf_op jit(solution)/shard_map/pallas_call | solution.py:123
  57.3 31.4 %collective-permute-done.2.refs_3_ = bf16[256,1024]{1,0:T(8,128)(2,1)} collective-permute-done((bf16[256,1024]{1,0:T(8,128)(2,1)}, bf16[256,1024]{1,0:T(8,128)(2,1)}, u32[]{:S(2)}, u32[]{:S(2)}) %collective-permute-start.2) | collective-permute-done | bytes 524320 | tf_op jit(solution)/shard_map/ppermute | solution.py:28
  88.7 12.6 %collective-permute-done.refs_1_ = bf16[256,1024]{1,0:T(8,128)(2,1)} collective-permute-done((bf16[256,1024]{1,0:T(8,128)(2,1)}, bf16[256,1024]{1,0:T(8,128)(2,1)}, u32[]{:S(2)}, u32[]{:S(2)}) %collective-permute-start) | collective-permute-done | bytes 524320 | tf_op jit(solution)/shard_map/ppermute | solution.py:28
  101.2 3.5 shard_map.175.other_ref.values_ref
  104.7 8.2 %all-to-all-done.1 = bf16[32,24,2048]{2,1,0:T(8,128)(2,1)S(1)} async-done(((bf16[32,24,2048]{2,1,0:T(8,128)(2,1)}), bf16[32,24,2048]{2,1,0:T(8,128)(2,1)S(1)}, u32[]{:S(2)}, u32[]{:S(2)}) %all-to-all-start.1) | async-done | bytes 3145760 | tf_op jit(solution)/shard_map/all_to_all | solution.py:557
  112.9 1.6 copy-done.32
  114.5 4.4 %shard_map.181 = (bf16[4,96,2048]{2,1,0:T(8,128)(2,1)}, bf16[4,96,2048]{2,1,0:T(8,128)(2,1)}) custom-call(s32[1]{0:T(128)} %bitcast.5.core_ref, bf16[96,192]{1,0:T(8,128)(2,1)} %shard_map.179.choose_ref, bf16[8,4,24,2048]{3,2,1,0:T(8,128)(2,1)} %bitcast.35, f32[1,8192]{1,0:T(1,128)} %bitcast.38), custom_call_target="tpu_custom_call" | custom-call | flops 301989888 | bytes 6291456 | tf_op jit(solution)/shard_map/pallas_call | solution.py:168
  118.9 3.6 all-to-all-start.2
  122.5 2.7 collective-permute-start.9
  126.0 33.4 %all-to-all-done.2 = bf16[4,96,2048]{2,1,0:T(8,128)(2,1)S(1)} async-done(((bf16[4,96,2048]{2,1,0:T(8,128)(2,1)}), bf16[4,96,2048]{2,1,0:T(8,128)(2,1)S(1)}, u32[]{:S(2)}, u32[]{:S(2)}) %all-to-all-start.2) | async-done | bytes 1572896 | tf_op jit(solution)/shard_map/all_to_all | solution.py:576
  161.8 3.7 shard_map.187.refs_4_.values_ref
  167.1 5.9 %collective-permute-start.3 = (bf16[1024,1024]{1,0:T(8,128)(2,1)}, bf16[1024,1024]{1,0:T(8,128)(2,1)}, u32[]{:S(2)}, u32[]{:S(2)}) collective-permute-start(bf16[1024,1024]{1,0:T(8,128)(2,1)} %shard_map.182.refs_3_), channel_id=1, source_target_pairs={{0,8},{8,16},{16,24},{1,9},{9,17},{17,25},{2,10},{10,18},{18,26},{... | collective-permute-start | bytes 6291464 | tf_op jit(solution)/shard_map/ppermute | solution.py:92
  173.0 1.9 collective-permute-start.4
  174.9 1.6 collective-permute-start.5
  176.5 7.4 %collective-permute-done.4.refs_1_ = bf16[96,2048]{1,0:T(8,128)(2,1)S(1)} collective-permute-done((bf16[96,2048]{1,0:T(8,128)(2,1)S(1)}, bf16[96,2048]{1,0:T(8,128)(2,1)S(1)}, u32[]{:S(2)}, u32[]{:S(2)}) %collective-permute-start.4) | collective-permute-done | bytes 393248 | tf_op jit(solution)/shard_map/ppermute | solution.py:28
  183.9 2.7 collective-permute-start.6
  186.6 8.3 %collective-permute-done.6.refs_3_ = bf16[96,2048]{1,0:T(8,128)(2,1)S(1)} collective-permute-done((bf16[96,2048]{1,0:T(8,128)(2,1)S(1)}, bf16[96,2048]{1,0:T(8,128)(2,1)S(1)}, u32[]{:S(2)}, u32[]{:S(2)}) %collective-permute-start.6) | collective-permute-done | bytes 393248 | tf_op jit(solution)/shard_map/ppermute | solution.py:28
  194.9 4.7 %shard_map.188.other_ref = bf16[384,1536]{1,0:T(8,128)(2,1)S(1)} custom-call(bf16[96,2048]{1,0:T(8,128)(2,1)S(1)} %copy-done.14, bf16[96,2048]{1,0:T(8,128)(2,1)S(1)} %collective-permute-done.4.refs_1_, bf16[96,2048]{1,0:T(8,128)(2,1)S(1)} %collective-permute-done.5.refs_2_, bf16[96,2048]{1,0:T(8,128)(2,1)S(1)} %collective-permute-done.6.refs_3_, ...), custom_call_target="tpu_custom_call" | custom-call | flops 2415919104 | bytes 6291456 | tf_op jit(solution)/shard_map/pallas_call | solution.py:243
  200.6 15.1 %collective-permute-done.13.values_ref = bf16[1024,1024]{1,0:T(8,128)(2,1)} collective-permute-done((bf16[1024,1024]{1,0:T(8,128)(2,1)}, bf16[1024,1024]{1,0:T(8,128)(2,1)}, u32[]{:S(2)}, u32[]{:S(2)}) %collective-permute-start.13) | collective-permute-done | bytes 2097184 | tf_op jit(solution)/shard_map/ppermute | solution.py:93
  217.2 2.0 collective-permute-start.11
  219.2 8.0 %collective-permute-start.28 = (bf16[384,1536]{1,0:T(8,128)(2,1)}, bf16[384,1536]{1,0:T(8,128)(2,1)S(1)}, u32[]{:S(2)}, u32[]{:S(2)}) collective-permute-start(bf16[384,1536]{1,0:T(8,128)(2,1)} %copy-done.12), channel_id=1, source_target_pairs={{0,8},{24,16},{1,9},{25,17},{2,10},{26,18},{3,11},{27,19},{4,12},{... | collective-permute-start | bytes 3538952 | tf_op jit(solution)/shard_map/ppermute | solution.py:60
  229.5 7.6 %collective-permute-done.25.refs_1_ = bf16[96,2048]{1,0:T(8,128)(2,1)S(1)} collective-permute-done((bf16[96,2048]{1,0:T(8,128)(2,1)}, bf16[96,2048]{1,0:T(8,128)(2,1)S(1)}, u32[]{:S(2)}, u32[]{:S(2)}) %collective-permute-start.25) | collective-permute-done | bytes 393248 | tf_op jit(solution)/shard_map/ppermute | solution.py:28
  237.2 1.6 collective-permute-start.27
  239.5 10.9 %collective-permute-done.27.refs_3_ = bf16[96,2048]{1,0:T(8,128)(2,1)S(1)} collective-permute-done((bf16[96,2048]{1,0:T(8,128)(2,1)}, bf16[96,2048]{1,0:T(8,128)(2,1)S(1)}, u32[]{:S(2)}, u32[]{:S(2)}) %collective-permute-start.27) | collective-permute-done | bytes 393248 | tf_op jit(solution)/shard_map/ppermute | solution.py:28
  251.3 4.7 %shard_map.199 = bf16[384,1536]{1,0:T(8,128)(2,1)S(1)} custom-call(bf16[96,2048]{1,0:T(8,128)(2,1)S(1)} %copy-done.22, bf16[96,2048]{1,0:T(8,128)(2,1)S(1)} %collective-permute-done.25.refs_1_, bf16[96,2048]{1,0:T(8,128)(2,1)S(1)} %collective-permute-done.26.refs_2_, bf16[96,2048]{1,0:T(8,128)(2,1)S(1)} %collective-permute-done.27.refs_3_, ...), custom_call_target="tpu_custom_call" | custom-call | flops 2415919104 | bytes 6291456 | tf_op jit(solution)/shard_map/pallas_call | solution.py:243
  256.3 1.6 collective-permute-start.29
  259.5 5.5 %collective-permute-done.14.other_ref.refs_5_ = bf16[1024,1024]{1,0:T(8,128)(2,1)} collective-permute-done((bf16[1024,1024]{1,0:T(8,128)(2,1)}, bf16[1024,1024]{1,0:T(8,128)(2,1)}, u32[]{:S(2)}, u32[]{:S(2)}) %collective-permute-start.14) | collective-permute-done | bytes 2097184 | tf_op jit(solution)/shard_map/ppermute | solution.py:93
  266.3 2.1 collective-permute-start.12
  268.4 2.9 collective-permute-start.24
  271.4 7.8 %collective-permute-done.24.refs_3_ = bf16[96,2048]{1,0:T(8,128)(2,1)S(1)} collective-permute-done((bf16[96,2048]{1,0:T(8,128)(2,1)S(1)}, bf16[96,2048]{1,0:T(8,128)(2,1)S(1)}, u32[]{:S(2)}, u32[]{:S(2)}) %collective-permute-start.24) | collective-permute-done | bytes 393248 | tf_op jit(solution)/shard_map/ppermute | solution.py:28
  279.1 2.6 collective-permute-start.16
  281.8 4.7 %shard_map.198 = bf16[384,1536]{1,0:T(8,128)(2,1)S(1)} custom-call(bf16[96,2048]{1,0:T(8,128)(2,1)S(1)} %copy-done.21, bf16[96,2048]{1,0:T(8,128)(2,1)S(1)} %collective-permute-done.22.refs_1_, bf16[96,2048]{1,0:T(8,128)(2,1)S(1)} %collective-permute-done.23.refs_2_, bf16[96,2048]{1,0:T(8,128)(2,1)S(1)} %collective-permute-done.24.refs_3_, ...), custom_call_target="tpu_custom_call" | custom-call | flops 2415919104 | bytes 6291456 | tf_op jit(solution)/shard_map/pallas_call | solution.py:243
  286.6 2.1 add_convert_fusion
  288.7 10.2 %collective-permute-start.30 = (bf16[384,1536]{1,0:T(8,128)(2,1)}, bf16[384,1536]{1,0:T(8,128)(2,1)S(1)}, u32[]{:S(2)}, u32[]{:S(2)}) collective-permute-start(bf16[384,1536]{1,0:T(8,128)(2,1)} %get-tuple-element.62), channel_id=1, source_target_pairs={{0,8},{8,16},{16,24},{1,9},{9,17},{17,25},{2,10},{10,18},{18,26},{... | collective-permute-start | bytes 3538952 | tf_op jit(solution)/shard_map/ppermute | solution.py:66
  302.0 2.6 dynamic-slice_bitcast_fusion.5
  304.6 5.4 %collective-permute-done.21.refs_2_ = bf16[96,2048]{1,0:T(8,128)(2,1)S(1)} collective-permute-done((bf16[96,2048]{1,0:T(8,128)(2,1)}, bf16[96,2048]{1,0:T(8,128)(2,1)S(1)}, u32[]{:S(2)}, u32[]{:S(2)}) %collective-permute-start.21) | collective-permute-done | bytes 393248 | tf_op jit(solution)/shard_map/ppermute | solution.py:28
  311.6 4.2 collective-permute-done.15.other_ref.refs_6_
  316.9 2.3 collective-permute-start.19
  321.2 1.9 copy-done.1
  324.1 4.8 %shard_map.196.values_ref = f32[384,1536]{1,0:T(8,128)S(1)} custom-call(bf16[96,2048]{1,0:T(8,128)(2,1)} %get-tuple-element.65.refs_0_, bf16[96,2048]{1,0:T(8,128)(2,1)S(1)} %copy-done.27, bf16[96,2048]{1,0:T(8,128)(2,1)S(1)} %copy-done.29, bf16[96,2048]{1,0:T(8,128)(2,1)S(1)} %copy-done.19, bf16[1024,1536]{1,0:T(8,128)(2,1)S(1)} %copy-done.1, ...), custom_call_target="tpu_custom_call" | custom-call | flops 2415919104 | bytes 6291456 | tf_op jit(solution)/shard_map/pallas_call | solution.py:243
  331.3 3.9 fusion.2.other_ref
  335.3 3.2 collective-permute-done.32.down_ref
  338.4 1.7 copy-done.7
  340.1 2.2 shard_map.200
  343.9 10.8 %shard_map.201.own_ref.values_ref = bf16[384,1024]{1,0:T(8,128)(2,1)} custom-call(s32[96]{0:T(128)} %lengths_ref.1, bf16[8,384,128]{2,1,0:T(8,128)(2,1)} %copy-done.25, bf16[384,512]{1,0:T(8,128)(2,1)} %copy-done.30, bf16[96,160,256]{2,1,0:T(8,128)(2,1)} %k_ref.1, bf16[96,160,256]{2,1,0:T(8,128)(2,1)} %v_ref.1), custom_call_target="tpu_custom_call" | custom-call | flops 1006632960 | bytes 15728640 | tf_op jit(solution)/shard_map/pallas_call | solution.py:395
  354.7 2.5 collective-permute-done.33.other_ref.values_ref
  360.4 4.6 %shard_map.207 = (bf16[384,1024]{1,0:T(8,128)(2,1)S(1)}, bf16[384,1024]{1,0:T(8,128)(2,1)}) custom-call(s32[1]{0:T(128)} %bitcast.21.info_ref, bf16[384,1024]{1,0:T(8,128)(2,1)S(1)} %copy-done.3, bf16[384,1024]{1,0:T(8,128)(2,1)S(1)} %copy-done.9, bf16[1024,1024]{1,0:T(8,128)(2,1)} %collective-permute-done.12.other_ref.refs_0_, ...), custom_call_target="tpu_custom_call" | custom-call | flops 1610612736 | bytes 6815744 | tf_op jit(solution)/shard_map/pallas_call | solution.py:443
  369.0 4.5 %shard_map.204 = (f32[384,1024]{1,0:T(8,128)S(1)}, bf16[384,1024]{1,0:T(8,128)(2,1)}) custom-call(s32[1]{0:T(128)} %bitcast.20.info_ref, bf16[384,1024]{1,0:T(8,128)(2,1)S(1)} %copy-done.4, bf16[384,1024]{1,0:T(8,128)(2,1)S(1)} %copy-done.10, bf16[1024,1024]{1,0:T(8,128)(2,1)} %collective-permute-done.12.other_ref.refs_0_, ...), custom_call_target="tpu_custom_call" | custom-call | flops 1610612736 | bytes 6815744 | tf_op jit(solution)/shard_map/pallas_call | solution.py:443
  375.3 4.5 %shard_map.202 = (bf16[384,1024]{1,0:T(8,128)(2,1)}, f32[384,1024]{1,0:T(8,128)S(1)}) custom-call(s32[1]{0:T(128)} %bitcast.19.info_ref, bf16[384,1024]{1,0:T(8,128)(2,1)S(1)} %copy-done.4, bf16[384,1024]{1,0:T(8,128)(2,1)S(1)} %copy-done.10, bf16[1024,1024]{1,0:T(8,128)(2,1)} %collective-permute-done.12.other_ref.refs_0_, ...), custom_call_target="tpu_custom_call" | custom-call | flops 1610612736 | bytes 6815744 | tf_op jit(solution)/shard_map/pallas_call | solution.py:443
  379.9 6.7 %collective-permute-done.38 = bf16[384,1024]{1,0:T(8,128)(2,1)} collective-permute-done((bf16[384,1024]{1,0:T(8,128)(2,1)}, bf16[384,1024]{1,0:T(8,128)(2,1)}, u32[]{:S(2)}, u32[]{:S(2)}) %collective-permute-start.38) | collective-permute-done | bytes 786464 | tf_op jit(solution)/shard_map/ppermute | solution.py:28
  386.6 2.3 add_convert_fusion.4
  388.9 1.9 collective-permute-start.39
  390.8 2.8 add_convert_fusion.5
  393.6 9.8 %collective-permute-done.35.other_ref = bf16[384,1024]{1,0:T(8,128)(2,1)} collective-permute-done((bf16[384,1024]{1,0:T(8,128)(2,1)}, bf16[384,1024]{1,0:T(8,128)(2,1)}, u32[]{:S(2)}, u32[]{:S(2)}) %collective-permute-start.35) | collective-permute-done | bytes 786464 | tf_op jit(solution)/shard_map/ppermute | solution.py:28
  405.7 2.2 shard_map.206
  407.9 12.4 %collective-permute-done.39 = bf16[384,1024]{1,0:T(8,128)(2,1)} collective-permute-done((bf16[384,1024]{1,0:T(8,128)(2,1)}, bf16[384,1024]{1,0:T(8,128)(2,1)}, u32[]{:S(2)}, u32[]{:S(2)}) %collective-permute-start.39) | collective-permute-done | bytes 786464 | tf_op jit(solution)/shard_map/ppermute | solution.py:28
  420.3 1.7 add_convert_fusion.3
  422.2 2.3 convert_add_fusion
  426.1 2.0 reshape.301
  (186 shorter events, 51.4 us)
Async XLA Ops:
  5.8 13.1 %all-to-all-start = ((s32[8,1,96]{2,1,0:T(1,128)}), s32[8,1,96]{2,1,0:T(1,128)S(1)}, u32[]{:S(2)}, u32[]{:S(2)}) async-start(s32[8,1,96]{2,1,0:T(1,128)} %all_to_all.13), calls=%async_computation | async-start | bytes 8192 | tf_op jit(solution)/shard_map/all_to_all | solution.py:546
  35.2 9.6 %copy-start.38 = (s32[96]{0:T(128)S(1)}, s32[96]{0:T(128)}, u32[]{:S(2)}) copy-start(s32[96]{0:T(128)} %lengths_ref.1) | copy-start | bytes 1156
  35.2 77.7 %all-to-all-start.1 = ((bf16[32,24,2048]{2,1,0:T(8,128)(2,1)}), bf16[32,24,2048]{2,1,0:T(8,128)(2,1)S(1)}, u32[]{:S(2)}, u32[]{:S(2)}) async-start(bf16[32,24,2048]{2,1,0:T(8,128)(2,1)} %bitcast.36), calls=%async_computation.1 | async-start | bytes 6291456 | tf_op jit(solution)/shard_map/all_to_all | solution.py:557
  41.3 47.4 %collective-permute-start.2 = (bf16[256,1024]{1,0:T(8,128)(2,1)}, bf16[256,1024]{1,0:T(8,128)(2,1)}, u32[]{:S(2)}, u32[]{:S(2)}) collective-permute-start(bf16[256,1024]{1,0:T(8,128)(2,1)} %get-tuple-element.36.other_ref), channel_id=1, source_target_pairs={{0,3},{1,2},{2,1},{3,0},{4,7},{5,6},{6,5},{7,4},{8,11},{9,10},{10,... | collective-permute-start | bytes 1572872 | tf_op jit(solution)/shard_map/ppermute | solution.py:28
  44.0 57.2 %collective-permute-start = (bf16[256,1024]{1,0:T(8,128)(2,1)}, bf16[256,1024]{1,0:T(8,128)(2,1)}, u32[]{:S(2)}, u32[]{:S(2)}) collective-permute-start(bf16[256,1024]{1,0:T(8,128)(2,1)} %get-tuple-element.34), channel_id=1, source_target_pairs={{0,1},{1,0},{2,3},{3,2},{4,5},{5,4},{6,7},{7,6},{8,9},{9,8},{10,11... | collective-permute-start | bytes 1572872 | tf_op jit(solution)/shard_map/ppermute | solution.py:28
  44.5 56.7 %collective-permute-start.1 = (bf16[256,1024]{1,0:T(8,128)(2,1)}, bf16[256,1024]{1,0:T(8,128)(2,1)}, u32[]{:S(2)}, u32[]{:S(2)}) collective-permute-start(bf16[256,1024]{1,0:T(8,128)(2,1)} %get-tuple-element.35), channel_id=1, source_target_pairs={{0,2},{1,3},{2,0},{3,1},{4,6},{5,7},{6,4},{7,5},{8,10},{9,11},{10,... | collective-permute-start | bytes 1572872 | tf_op jit(solution)/shard_map/ppermute | solution.py:28
  112.9 1.6 copy-start.32
  118.9 40.6 %all-to-all-start.2 = ((bf16[4,96,2048]{2,1,0:T(8,128)(2,1)}), bf16[4,96,2048]{2,1,0:T(8,128)(2,1)S(1)}, u32[]{:S(2)}, u32[]{:S(2)}) async-start(bf16[4,96,2048]{2,1,0:T(8,128)(2,1)} %get-tuple-element.38.other_ref), calls=%async_computation.2 | async-start | bytes 3145728 | tf_op jit(solution)/shard_map/all_to_all | solution.py:576
  122.5 38.2 %collective-permute-start.9 = (bf16[256,1536]{1,0:T(8,128)(2,1)}, bf16[256,1536]{1,0:T(8,128)(2,1)S(1)}, u32[]{:S(2)}, u32[]{:S(2)}) collective-permute-start(bf16[256,1536]{1,0:T(8,128)(2,1)} %shard_map.186), channel_id=1, source_target_pairs={{0,3},{1,2},{2,1},{3,0},{4,7},{5,6},{6,5},{7,4},{8,11},{9,10},{10,... | collective-permute-start | bytes 2359304 | tf_op jit(solution)/shard_map/ppermute | solution.py:28
  125.2 35.5 %collective-permute-start.8 = (bf16[256,1536]{1,0:T(8,128)(2,1)}, bf16[256,1536]{1,0:T(8,128)(2,1)S(1)}, u32[]{:S(2)}, u32[]{:S(2)}) collective-permute-start(bf16[256,1536]{1,0:T(8,128)(2,1)} %shard_map.185), channel_id=1, source_target_pairs={{0,2},{1,3},{2,0},{3,1},{4,6},{5,7},{6,4},{7,5},{8,10},{9,11},{10,... | collective-permute-start | bytes 2359304 | tf_op jit(solution)/shard_map/ppermute | solution.py:28
  125.7 35.0 %collective-permute-start.7 = (bf16[256,1536]{1,0:T(8,128)(2,1)}, bf16[256,1536]{1,0:T(8,128)(2,1)}, u32[]{:S(2)}, u32[]{:S(2)}) collective-permute-start(bf16[256,1536]{1,0:T(8,128)(2,1)} %shard_map.184), channel_id=1, source_target_pairs={{0,1},{1,0},{2,3},{3,2},{4,5},{5,4},{6,7},{7,6},{8,9},{9,8},{10,11... | collective-permute-start | bytes 2359304 | tf_op jit(solution)/shard_map/ppermute | solution.py:28
  165.5 7.5 %copy-start.14 = (bf16[96,2048]{1,0:T(8,128)(2,1)S(1)}, bf16[96,2048]{1,0:T(8,128)(2,1)}, u32[]{:S(2)}) copy-start(bf16[96,2048]{1,0:T(8,128)(2,1)} %get-tuple-element.66.other_ref.refs_0_) | copy-start | bytes 1179652
  165.5 29.4 %copy-start = (bf16[1024,1536]{1,0:T(8,128)(2,1)S(1)}, bf16[1024,1536]{1,0:T(8,128)(2,1)}, u32[]{:S(2)}) copy-start(bf16[1024,1536]{1,0:T(8,128)(2,1)} %shard_map.187.refs_4_.values_ref) | copy-start | bytes 9437188
  165.5 29.4 %collective-permute-start.10 = (bf16[1024,1536]{1,0:T(8,128)(2,1)}, bf16[1024,1536]{1,0:T(8,128)(2,1)}, u32[]{:S(2)}, u32[]{:S(2)}) collective-permute-start(bf16[1024,1536]{1,0:T(8,128)(2,1)} %shard_map.187.refs_4_.values_ref), channel_id=1, source_target_pairs={{0,4},{4,0},{1,5},{5,1},{2,6},{6,2},{3,7},{7,3},{8,12},{12,8},{9,1... | collective-permute-start | bytes 9437192 | tf_op jit(solution)/shard_map/ppermute | solution.py:587
  165.5 50.2 %collective-permute-start.13 = (bf16[1024,1024]{1,0:T(8,128)(2,1)}, bf16[1024,1024]{1,0:T(8,128)(2,1)}, u32[]{:S(2)}, u32[]{:S(2)}) collective-permute-start(bf16[1024,1024]{1,0:T(8,128)(2,1)} %shard_map.182.refs_3_), channel_id=1, source_target_pairs={{8,0},{16,8},{24,16},{9,1},{17,9},{25,17},{10,2},{18,10},{26,18},{... | collective-permute-start | bytes 6291464 | tf_op jit(solution)/shard_map/ppermute | solution.py:93
  167.1 50.1 %collective-permute-start.3 = (bf16[1024,1024]{1,0:T(8,128)(2,1)}, bf16[1024,1024]{1,0:T(8,128)(2,1)}, u32[]{:S(2)}, u32[]{:S(2)}) collective-permute-start(bf16[1024,1024]{1,0:T(8,128)(2,1)} %shard_map.182.refs_3_), channel_id=1, source_target_pairs={{0,8},{8,16},{16,24},{1,9},{9,17},{17,25},{2,10},{10,18},{18,26},{... | collective-permute-start | bytes 6291464 | tf_op jit(solution)/shard_map/ppermute | solution.py:92
  173.0 10.9 %collective-permute-start.4 = (bf16[96,2048]{1,0:T(8,128)(2,1)S(1)}, bf16[96,2048]{1,0:T(8,128)(2,1)S(1)}, u32[]{:S(2)}, u32[]{:S(2)}) collective-permute-start(bf16[96,2048]{1,0:T(8,128)(2,1)S(1)} %copy-done.14), channel_id=1, source_target_pairs={{0,1},{1,0},{2,3},{3,2},{4,5},{5,4},{6,7},{7,6},{8,9},{9,8},{10,11... | collective-permute-start | bytes 1179656 | tf_op jit(solution)/shard_map/ppermute | solution.py:28
  174.9 11.7 %collective-permute-start.5 = (bf16[96,2048]{1,0:T(8,128)(2,1)S(1)}, bf16[96,2048]{1,0:T(8,128)(2,1)S(1)}, u32[]{:S(2)}, u32[]{:S(2)}) collective-permute-start(bf16[96,2048]{1,0:T(8,128)(2,1)S(1)} %copy-done.14), channel_id=1, source_target_pairs={{0,2},{1,3},{2,0},{3,1},{4,6},{5,7},{6,4},{7,5},{8,10},{9,11},{10,... | collective-permute-start | bytes 1179656 | tf_op jit(solution)/shard_map/ppermute | solution.py:28
  183.9 11.0 %collective-permute-start.6 = (bf16[96,2048]{1,0:T(8,128)(2,1)S(1)}, bf16[96,2048]{1,0:T(8,128)(2,1)S(1)}, u32[]{:S(2)}, u32[]{:S(2)}) collective-permute-start(bf16[96,2048]{1,0:T(8,128)(2,1)S(1)} %copy-done.14), channel_id=1, source_target_pairs={{0,3},{1,2},{2,1},{3,0},{4,7},{5,6},{6,5},{7,4},{8,11},{9,10},{10,... | collective-permute-start | bytes 1179656 | tf_op jit(solution)/shard_map/ppermute | solution.py:28
  215.8 23.0 %copy-start.20 = (bf16[96,2048]{1,0:T(8,128)(2,1)S(1)}, bf16[96,2048]{1,0:T(8,128)(2,1)}, u32[]{:S(2)}) copy-start(bf16[96,2048]{1,0:T(8,128)(2,1)} %get-tuple-element.63.refs_0_) | copy-start | bytes 1179652
  215.8 49.3 %collective-permute-start.14 = (bf16[1024,1024]{1,0:T(8,128)(2,1)}, bf16[1024,1024]{1,0:T(8,128)(2,1)}, u32[]{:S(2)}, u32[]{:S(2)}) collective-permute-start(bf16[1024,1024]{1,0:T(8,128)(2,1)} %shard_map.191.refs_4_), channel_id=1, source_target_pairs={{8,0},{16,8},{9,1},{17,9},{10,2},{18,10},{11,3},{19,11},{12,4},{20... | collective-permute-start | bytes 6291464 | tf_op jit(solution)/shard_map/ppermute | solution.py:93
  217.2 49.1 %collective-permute-start.11 = (bf16[1024,1024]{1,0:T(8,128)(2,1)}, bf16[1024,1024]{1,0:T(8,128)(2,1)}, u32[]{:S(2)}, u32[]{:S(2)}) collective-permute-start(bf16[1024,1024]{1,0:T(8,128)(2,1)} %shard_map.189.refs_2_), channel_id=1, source_target_pairs={{8,16},{16,24},{9,17},{17,25},{10,18},{18,26},{11,19},{19,27},{12,... | collective-permute-start | bytes 6291464 | tf_op jit(solution)/shard_map/ppermute | solution.py:92
  219.2 36.8 %collective-permute-start.28 = (bf16[384,1536]{1,0:T(8,128)(2,1)}, bf16[384,1536]{1,0:T(8,128)(2,1)S(1)}, u32[]{:S(2)}, u32[]{:S(2)}) collective-permute-start(bf16[384,1536]{1,0:T(8,128)(2,1)} %copy-done.12), channel_id=1, source_target_pairs={{0,8},{24,16},{1,9},{25,17},{2,10},{26,18},{3,11},{27,19},{4,12},{... | collective-permute-start | bytes 3538952 | tf_op jit(solution)/shard_map/ppermute | solution.py:60
  227.1 10.0 %collective-permute-start.25 = (bf16[96,2048]{1,0:T(8,128)(2,1)}, bf16[96,2048]{1,0:T(8,128)(2,1)S(1)}, u32[]{:S(2)}, u32[]{:S(2)}) collective-permute-start(bf16[96,2048]{1,0:T(8,128)(2,1)} %get-tuple-element.64.refs_0_), channel_id=1, source_target_pairs={{0,1},{1,0},{2,3},{3,2},{4,5},{5,4},{6,7},{7,6},{8,9},{9,8},{10,11... | collective-permute-start | bytes 1179656 | tf_op jit(solution)/shard_map/ppermute | solution.py:28
  228.3 10.4 %collective-permute-start.26 = (bf16[96,2048]{1,0:T(8,128)(2,1)}, bf16[96,2048]{1,0:T(8,128)(2,1)S(1)}, u32[]{:S(2)}, u32[]{:S(2)}) collective-permute-start(bf16[96,2048]{1,0:T(8,128)(2,1)} %get-tuple-element.64.refs_0_), channel_id=1, source_target_pairs={{0,2},{1,3},{2,0},{3,1},{4,6},{5,7},{6,4},{7,5},{8,10},{9,11},{10,... | collective-permute-start | bytes 1179656 | tf_op jit(solution)/shard_map/ppermute | solution.py:28
  237.2 13.2 %collective-permute-start.27 = (bf16[96,2048]{1,0:T(8,128)(2,1)}, bf16[96,2048]{1,0:T(8,128)(2,1)S(1)}, u32[]{:S(2)}, u32[]{:S(2)}) collective-permute-start(bf16[96,2048]{1,0:T(8,128)(2,1)} %get-tuple-element.64.refs_0_), channel_id=1, source_target_pairs={{0,3},{1,2},{2,1},{3,0},{4,7},{5,6},{6,5},{7,4},{8,11},{9,10},{10,... | collective-permute-start | bytes 1179656 | tf_op jit(solution)/shard_map/ppermute | solution.py:28
  238.8 19.9 %collective-permute-start.22 = (bf16[96,2048]{1,0:T(8,128)(2,1)S(1)}, bf16[96,2048]{1,0:T(8,128)(2,1)S(1)}, u32[]{:S(2)}, u32[]{:S(2)}) collective-permute-start(bf16[96,2048]{1,0:T(8,128)(2,1)S(1)} %copy-done.20), channel_id=1, source_target_pairs={{0,1},{1,0},{2,3},{3,2},{4,5},{5,4},{6,7},{7,6},{8,9},{9,8},{10,11... | collective-permute-start | bytes 1179656 | tf_op jit(solution)/shard_map/ppermute | solution.py:28
  256.0 25.8 %copy-start.21 = (bf16[96,2048]{1,0:T(8,128)(2,1)S(1)}, bf16[96,2048]{1,0:T(8,128)(2,1)}, u32[]{:S(2)}) copy-start(bf16[96,2048]{1,0:T(8,128)(2,1)} %get-tuple-element.63.refs_0_) | copy-start | bytes 1179652
  256.3 30.2 %collective-permute-start.29 = (bf16[384,1536]{1,0:T(8,128)(2,1)S(1)}, bf16[384,1536]{1,0:T(8,128)(2,1)S(1)}, u32[]{:S(2)}, u32[]{:S(2)}) collective-permute-start(bf16[384,1536]{1,0:T(8,128)(2,1)S(1)} %add_convert_fusion.2), channel_id=1, source_target_pairs={{0,8},{8,16},{1,9},{9,17},{2,10},{10,18},{3,11},{11,19},{4,12},{12... | collective-permute-start | bytes 3538952 | tf_op jit(solution)/shard_map/ppermute | solution.py:62
  257.9 28.7 %collective-permute-start.31 = (bf16[384,1536]{1,0:T(8,128)(2,1)S(1)}, bf16[384,1536]{1,0:T(8,128)(2,1)S(1)}, u32[]{:S(2)}, u32[]{:S(2)}) collective-permute-start(bf16[384,1536]{1,0:T(8,128)(2,1)S(1)} %add_convert_fusion.2), channel_id=1, source_target_pairs={{24,16},{16,8},{25,17},{17,9},{26,18},{18,10},{27,19},{19,11},{28,... | collective-permute-start | bytes 3538952 | tf_op jit(solution)/shard_map/ppermute | solution.py:63
  258.6 9.8 %collective-permute-start.23 = (bf16[96,2048]{1,0:T(8,128)(2,1)S(1)}, bf16[96,2048]{1,0:T(8,128)(2,1)S(1)}, u32[]{:S(2)}, u32[]{:S(2)}) collective-permute-start(bf16[96,2048]{1,0:T(8,128)(2,1)S(1)} %copy-done.20), channel_id=1, source_target_pairs={{0,2},{1,3},{2,0},{3,1},{4,6},{5,7},{6,4},{7,5},{8,10},{9,11},{10,... | collective-permute-start | bytes 1179656 | tf_op jit(solution)/shard_map/ppermute | solution.py:28
  265.0 50.8 %collective-permute-start.15 = (bf16[1024,1024]{1,0:T(8,128)(2,1)}, bf16[1024,1024]{1,0:T(8,128)(2,1)}, u32[]{:S(2)}, u32[]{:S(2)}) collective-permute-start(bf16[1024,1024]{1,0:T(8,128)(2,1)} %collective-permute-done.14.other_ref.refs_5_), channel_id=1, source_target_pairs={{8,0},{9,1},{10,2},{11,3},{12,4},{13,5},{14,6},{15,7}} | collective-permute-start | bytes 6291464 | tf_op jit(solution)/shard_map/ppermute | solution.py:93
  266.3 50.6 %collective-permute-start.12 = (bf16[1024,1024]{1,0:T(8,128)(2,1)}, bf16[1024,1024]{1,0:T(8,128)(2,1)}, u32[]{:S(2)}, u32[]{:S(2)}) collective-permute-start(bf16[1024,1024]{1,0:T(8,128)(2,1)} %collective-permute-done.11.other_ref.refs_1_), channel_id=1, source_target_pairs={{16,24},{17,25},{18,26},{19,27},{20,28},{21,29},{22,30},{23,31}} | collective-permute-start | bytes 6291464 | tf_op jit(solution)/shard_map/ppermute | solution.py:92
  268.4 10.7 %collective-permute-start.24 = (bf16[96,2048]{1,0:T(8,128)(2,1)S(1)}, bf16[96,2048]{1,0:T(8,128)(2,1)S(1)}, u32[]{:S(2)}, u32[]{:S(2)}) collective-permute-start(bf16[96,2048]{1,0:T(8,128)(2,1)S(1)} %copy-done.20), channel_id=1, source_target_pairs={{0,3},{1,2},{2,1},{3,0},{4,7},{5,6},{6,5},{7,4},{8,11},{9,10},{10,... | collective-permute-start | bytes 1179656 | tf_op jit(solution)/shard_map/ppermute | solution.py:28
  279.1 7.4 %copy-start.13 = (bf16[384,1536]{1,0:T(8,128)(2,1)S(1)}, bf16[384,1536]{1,0:T(8,128)(2,1)}, u32[]{:S(2)}) copy-start(bf16[384,1536]{1,0:T(8,128)(2,1)} %copy-done.12) | copy-start | bytes 3538948
  279.1 19.8 %collective-permute-start.16 = (bf16[96,2048]{1,0:T(8,128)(2,1)}, bf16[96,2048]{1,0:T(8,128)(2,1)S(1)}, u32[]{:S(2)}, u32[]{:S(2)}) collective-permute-start(bf16[96,2048]{1,0:T(8,128)(2,1)} %get-tuple-element.65.refs_0_), channel_id=1, source_target_pairs={{0,3},{1,2},{2,1},{3,0},{4,7},{5,6},{6,5},{7,4},{8,11},{9,10},{10,... | collective-permute-start | bytes 1179656 | tf_op jit(solution)/shard_map/ppermute | solution.py:28
  286.5 13.7 %collective-permute-start.20 = (bf16[96,2048]{1,0:T(8,128)(2,1)}, bf16[96,2048]{1,0:T(8,128)(2,1)S(1)}, u32[]{:S(2)}, u32[]{:S(2)}) collective-permute-start(bf16[96,2048]{1,0:T(8,128)(2,1)} %get-tuple-element.65.refs_0_), channel_id=1, source_target_pairs={{0,1},{1,0},{2,3},{3,2},{4,5},{5,4},{6,7},{7,6},{8,9},{9,8},{10,11... | collective-permute-start | bytes 1179656 | tf_op jit(solution)/shard_map/ppermute | solution.py:28
  288.7 46.5 %collective-permute-start.30 = (bf16[384,1536]{1,0:T(8,128)(2,1)}, bf16[384,1536]{1,0:T(8,128)(2,1)S(1)}, u32[]{:S(2)}, u32[]{:S(2)}) collective-permute-start(bf16[384,1536]{1,0:T(8,128)(2,1)} %get-tuple-element.62), channel_id=1, source_target_pairs={{0,8},{8,16},{16,24},{1,9},{9,17},{17,25},{2,10},{10,18},{18,26},{... | collective-permute-start | bytes 3538952 | tf_op jit(solution)/shard_map/ppermute | solution.py:66
  298.9 3.1 copy-start.18
  298.9 39.5 %collective-permute-start.32 = (bf16[384,1536]{1,0:T(8,128)(2,1)}, bf16[384,1536]{1,0:T(8,128)(2,1)S(1)}, u32[]{:S(2)}, u32[]{:S(2)}) collective-permute-start(bf16[384,1536]{1,0:T(8,128)(2,1)} %get-tuple-element.61), channel_id=1, source_target_pairs={{24,16},{16,8},{8,0},{25,17},{17,9},{9,1},{26,18},{18,10},{10,2},{... | collective-permute-start | bytes 3538952 | tf_op jit(solution)/shard_map/ppermute | solution.py:69
  301.0 9.0 %collective-permute-start.21 = (bf16[96,2048]{1,0:T(8,128)(2,1)}, bf16[96,2048]{1,0:T(8,128)(2,1)S(1)}, u32[]{:S(2)}, u32[]{:S(2)}) collective-permute-start(bf16[96,2048]{1,0:T(8,128)(2,1)} %get-tuple-element.65.refs_0_), channel_id=1, source_target_pairs={{0,2},{1,3},{2,0},{3,1},{4,6},{5,7},{6,4},{7,5},{8,10},{9,11},{10,... | collective-permute-start | bytes 1179656 | tf_op jit(solution)/shard_map/ppermute | solution.py:28
  310.7 19.6 %collective-permute-start.17 = (bf16[96,2048]{1,0:T(8,128)(2,1)}, bf16[96,2048]{1,0:T(8,128)(2,1)}, u32[]{:S(2)}, u32[]{:S(2)}) collective-permute-start(bf16[96,2048]{1,0:T(8,128)(2,1)} %get-tuple-element.70), channel_id=1, source_target_pairs={{0,1},{1,0},{2,3},{3,2},{4,5},{5,4},{6,7},{7,6},{8,9},{9,8},{10,11... | collective-permute-start | bytes 1179656 | tf_op jit(solution)/shard_map/ppermute | solution.py:28
  315.8 14.8 %collective-permute-start.18 = (bf16[96,2048]{1,0:T(8,128)(2,1)}, bf16[96,2048]{1,0:T(8,128)(2,1)}, u32[]{:S(2)}, u32[]{:S(2)}) collective-permute-start(bf16[96,2048]{1,0:T(8,128)(2,1)} %get-tuple-element.69), channel_id=1, source_target_pairs={{0,2},{1,3},{2,0},{3,1},{4,6},{5,7},{6,4},{7,5},{8,10},{9,11},{10,... | collective-permute-start | bytes 1179656 | tf_op jit(solution)/shard_map/ppermute | solution.py:28
  316.9 13.6 %collective-permute-start.19 = (bf16[96,2048]{1,0:T(8,128)(2,1)}, bf16[96,2048]{1,0:T(8,128)(2,1)}, u32[]{:S(2)}, u32[]{:S(2)}) collective-permute-start(bf16[96,2048]{1,0:T(8,128)(2,1)} %get-tuple-element.68), channel_id=1, source_target_pairs={{0,3},{1,2},{2,1},{3,0},{4,7},{5,6},{6,5},{7,4},{8,11},{9,10},{10,... | collective-permute-start | bytes 1179656 | tf_op jit(solution)/shard_map/ppermute | solution.py:28
  321.2 1.9 copy-start.1
  328.9 1.4 copy-start.6
  335.2 3.2 copy-start.15
  335.2 3.2 copy-start.16
  335.2 3.2 copy-start.17
  338.4 1.7 copy-start.7
  343.9 14.2 %copy-start.2 = (bf16[1024,1024]{1,0:T(8,128)(2,1)S(1)}, bf16[1024,1024]{1,0:T(8,128)(2,1)}, u32[]{:S(2)}) copy-start(bf16[1024,1024]{1,0:T(8,128)(2,1)} %shard_map.182.refs_3_) | copy-start | bytes 6291460
  354.7 2.5 collective-permute-start.33
  360.4 7.5 %copy-start.4 = (bf16[384,1024]{1,0:T(8,128)(2,1)S(1)}, bf16[384,1024]{1,0:T(8,128)(2,1)}, u32[]{:S(2)}) copy-start(bf16[384,1024]{1,0:T(8,128)(2,1)} %shard_map.201.own_ref.values_ref) | copy-start | bytes 2359300
  365.9 20.7 %collective-permute-start.38 = (bf16[384,1024]{1,0:T(8,128)(2,1)}, bf16[384,1024]{1,0:T(8,128)(2,1)}, u32[]{:S(2)}, u32[]{:S(2)}) collective-permute-start(bf16[384,1024]{1,0:T(8,128)(2,1)} %get-tuple-element.52), channel_id=1, source_target_pairs={{0,2},{1,3},{2,0},{3,1},{4,6},{5,7},{6,4},{7,5},{8,10},{9,11},{10,... | collective-permute-start | bytes 2359304 | tf_op jit(solution)/shard_map/ppermute | solution.py:28
  367.0 23.8 %collective-permute-start.36 = (bf16[384,1024]{1,0:T(8,128)(2,1)}, bf16[384,1024]{1,0:T(8,128)(2,1)}, u32[]{:S(2)}, u32[]{:S(2)}) collective-permute-start(bf16[384,1024]{1,0:T(8,128)(2,1)} %copy-done.31), channel_id=1, source_target_pairs={{0,1},{1,0},{2,3},{3,2},{4,5},{5,4},{6,7},{7,6},{8,9},{9,8},{10,11... | collective-permute-start | bytes 2359304 | tf_op jit(solution)/shard_map/ppermute | solution.py:28
  373.6 1.1 copy-start.23
  374.7 28.7 %collective-permute-start.35 = (bf16[384,1024]{1,0:T(8,128)(2,1)}, bf16[384,1024]{1,0:T(8,128)(2,1)}, u32[]{:S(2)}, u32[]{:S(2)}) collective-permute-start(bf16[384,1024]{1,0:T(8,128)(2,1)} %get-tuple-element.46), channel_id=1, source_target_pairs={{0,2},{1,3},{2,0},{3,1},{4,6},{5,7},{6,4},{7,5},{8,10},{9,11},{10,... | collective-permute-start | bytes 2359304 | tf_op jit(solution)/shard_map/ppermute | solution.py:28
  379.8 24.8 %collective-permute-start.34 = (bf16[384,1024]{1,0:T(8,128)(2,1)}, bf16[384,1024]{1,0:T(8,128)(2,1)}, u32[]{:S(2)}, u32[]{:S(2)}) collective-permute-start(bf16[384,1024]{1,0:T(8,128)(2,1)} %get-tuple-element.45), channel_id=1, source_target_pairs={{0,1},{1,0},{2,3},{3,2},{4,5},{5,4},{6,7},{7,6},{8,9},{9,8},{10,11... | collective-permute-start | bytes 2359304 | tf_op jit(solution)/shard_map/ppermute | solution.py:28
  388.9 31.5 %collective-permute-start.39 = (bf16[384,1024]{1,0:T(8,128)(2,1)}, bf16[384,1024]{1,0:T(8,128)(2,1)}, u32[]{:S(2)}, u32[]{:S(2)}) collective-permute-start(bf16[384,1024]{1,0:T(8,128)(2,1)} %add_convert_fusion.4), channel_id=1, source_target_pairs={{0,1},{1,0},{2,3},{3,2},{4,5},{5,4},{6,7},{7,6},{8,9},{9,8},{10,11... | collective-permute-start | bytes 2359304 | tf_op jit(solution)/shard_map/ppermute | solution.py:28
  393.6 28.6 %collective-permute-start.37 = (bf16[384,1024]{1,0:T(8,128)(2,1)}, bf16[384,1024]{1,0:T(8,128)(2,1)}, u32[]{:S(2)}, u32[]{:S(2)}) collective-permute-start(bf16[384,1024]{1,0:T(8,128)(2,1)} %add_convert_fusion.5), channel_id=1, source_target_pairs={{0,2},{1,3},{2,0},{3,1},{4,6},{5,7},{6,4},{7,5},{8,10},{9,11},{10,... | collective-permute-start | bytes 2359304 | tf_op jit(solution)/shard_map/ppermute | solution.py:28
  403.4 1.2 copy-start.11
  407.9 14.1 %copy-start.24 = (f32[384,1024]{1,0:T(8,128)}, f32[384,1024]{1,0:T(8,128)S(1)}, u32[]{:S(2)}) copy-start(f32[384,1024]{1,0:T(8,128)S(1)} %get-tuple-element.47) | copy-start | bytes 4718596
  422.1 2.4 collective-permute-start.40
  422.2 2.8 copy-start.33
  (19 other events, 18.3 us)
